TPU v7x, 512 devices: a whole 4x4x16 slice. The times are simulated.
512 devices in a mesh: tm: 8 (over y, core), space: 64 (over z, x).
Axes of the slice: x: 4, y: 4, z: 16, core: 2. Of those that a mesh axis runs over, the one named last changes fastest.
Arguments:
- bases: bfloat16 [8, 524288, 128], P('tm', 'space'), may hold values from -12 to 12
- sing_values: float32 [8, 128], P('tm'), may hold values from 0.5 to 4
Outputs:
- merged_bases: bfloat16 [8, 524288, 128], P('tm', 'space')
- merged_values: float32 [8, 128], P('tm')
All inputs are finite; a program needn't handle non-finite values.
Results may differ from a plain program's by a relative error of at most 0.0051.
Values may be sent and summed in bfloat16 or wider, within the bound.
No kernel may reach another device: no remote copies, remote signals or barrier semaphores. Data moves between devices by JAX's collectives and lax.ppermute only.
A program may use at most 64 MiB of HBM per device.

v0:
```python
import jax
import jax.numpy as jnp
from jax import lax
from jax.sharding import PartitionSpec as P

ITERS = 3
NS_STEPS = 6


def partner(value, axis, stride):
    return lax.ppermute(value, axis, [(i, i ^ 1 << stride) for i in range(lax.axis_size(axis))])


def polar_iterate(gram, width):
    eye = jnp.eye(width, dtype=jnp.float32)
    start = jnp.concatenate([eye, eye], axis=0) / jnp.sqrt(jnp.float32(2.0))
    for outer in range(ITERS):
        y = jnp.dot(gram, start, precision=lax.Precision.HIGHEST)
        y = y / jnp.sqrt(jnp.sum(y * y) + 1e-06)
        for inner in range(NS_STEPS):
            inner_prod = jnp.dot(y.T, y, precision=lax.Precision.HIGHEST)
            y = 1.5 * y - 0.5 * jnp.dot(y, inner_prod, precision=lax.Precision.HIGHEST)
        start = y
    return start


def local(bases, sing_values):
    width = bases.shape[2]
    rows = bases.shape[1]
    points_all = rows * lax.axis_size("space")
    own = (bases[0].astype(jnp.float32) * sing_values[0][None, :]).astype(jnp.bfloat16)
    other = partner(own, "tm", 0)
    stacked = jnp.concatenate([own, other], axis=1)
    local_gram = lax.dot_general(
        stacked, stacked, (((0,), (0,)), ((), ())), preferred_element_type=jnp.float32
    )
    gram = lax.psum(local_gram, "space")
    rotation = polar_iterate(gram, width).astype(jnp.bfloat16)
    merged = jnp.dot(own, rotation[:width], preferred_element_type=jnp.float32)
    merged = merged + jnp.dot(other, rotation[width:], preferred_element_type=jnp.float32)
    squares = lax.psum(jnp.sum(merged * merged, axis=0), "space")
    values = jnp.sqrt(squares / points_all + 1e-06)
    merged_bases = (merged / values[None, :]).astype(jnp.bfloat16)
    return (merged_bases[None], values[None])


def solution(mesh):
    in_specs = (P("tm", "space", None), P("tm", None))
    out_specs = (P("tm", "space", None), P("tm", None))
    return jax.shard_map(local, mesh=mesh, in_specs=in_specs, out_specs=out_specs, check_vma=False)
```

profile of v0, /device:TPU:8, one launch (start us, length us, event | category | flops | bytes accessed | tf_op | source)
XLA Modules:
  0.0 459.4 jit_solution(5780209339751615930)
XLA Ops:
  7.2 0.0 all-reduce.2.cloned.1.call-start
  7.2 2.0 fusion.4
  9.2 1.9 collective-permute-start
  11.1 4.1 collective-permute-done
  15.3 0.0 copy-start
  15.3 1.3 copy-done
  16.6 2.0 fusion
  18.6 0.0 all-reduce.2.cloned.1.call-update
  18.6 267.1 %all-reduce.2.cloned.1.call-done = f32[256,256]{1,0:T(8,128)} async-done(((f32[256,256]{1,0:T(8,128)}), f32[256,256]{1,0:T(8,128)}) %all-reduce.2.cloned.1.call-update) | async-done | bytes 262160 | tf_op jit(solution)/shard_map/psum | solution.py:37
  285.8 0.0 copy-start.2
  285.8 2.0 multiply_reduce_fusion.3
  288.5 0.4 fusion.32
  288.9 0.3 fusion.6
  289.1 0.4 fusion.43
  289.5 0.3 fusion.7
  289.8 0.4 fusion.44
  290.2 0.3 fusion.8
  290.4 0.4 fusion.45
  290.8 0.3 fusion.9
  291.1 0.4 fusion.46
  291.5 0.3 fusion.10
  291.8 0.4 fusion.47
  292.2 0.3 fusion.11
  292.4 0.0 copy-done.2
  292.4 1.0 multiply_reduce_fusion.2
  294.1 0.4 fusion.33
  294.5 0.3 fusion.12
  294.8 0.4 fusion.48
  295.2 0.3 fusion.13
  295.4 0.4 fusion.49
  295.8 0.3 fusion.14
  296.1 0.4 fusion.50
  296.5 0.3 fusion.15
  296.8 0.4 fusion.51
  297.1 0.3 fusion.16
  297.4 0.4 fusion.52
  297.8 0.3 fusion.17
  298.1 1.0 multiply_reduce_fusion.1
  299.8 0.4 fusion.34
  300.1 0.3 fusion.18
  300.4 0.4 fusion.53
  300.8 0.3 fusion.19
  301.1 0.4 fusion.54
  301.5 0.3 fusion.20
  301.7 0.4 fusion.55
  302.1 0.3 fusion.21
  302.4 0.4 fusion.56
  302.8 0.3 fusion.22
  303.1 0.6 fusion.57
  303.6 0.3 fusion.24
  303.9 0.0 copy-start.1
  303.9 0.7 fusion.36
  304.6 0.9 copy-done.1
  305.5 3.1 multiply_reduce_fusion
  308.6 139.6 %psum.15 = f32[128]{0:T(128)S(1)} all-reduce(f32[128]{0:T(128)S(1)} %get-tuple-element.10), channel_id=1, replica_groups=mesh['tm'=8,'space'=64] {'space'}, use_global_device_ids=true, to_apply=%region_5.0 | all-reduce | flops 128 | bytes 1024 | tf_op jit(solution)/shard_map/psum | solution.py:41
  448.2 0.5 fusion.42
  448.7 3.8 fusion.5
  (1 shorter events, 0.0 us)
Async XLA Ops:
  7.2 278.6 %all-reduce.2.cloned.1.call-start = ((), (), s32[]{:S(2)}) async-start(), calls=%async_computation | async-start | bytes 524288 | tf_op jit(solution)/shard_map/psum | solution.py:37
  9.2 6.1 %collective-permute-start = (bf16[8192,128]{1,0:T(8,128)(2,1)S(1)}, bf16[8192,128]{1,0:T(8,128)(2,1)S(1)}, u32[]{:S(2)}, u32[]{:S(2)}) collective-permute-start(bf16[8192,128]{1,0:T(8,128)(2,1)S(1)} %fusion.4), channel_id=1, source_target_pairs={{0,64},{64,0},{128,192},{192,128},{256,320},{320,256},{384,448},{4... | collective-permute-start | bytes 6291464 | tf_op jit(solution)/shard_map/ppermute | solution.py:11
  15.3 1.3 copy-start
  285.8 6.7 %copy-start.2 = (f32[256,256]{1,0:T(8,128)S(1)}, f32[256,256]{1,0:T(8,128)}, u32[]{:S(2)}) copy-start(f32[256,256]{1,0:T(8,128)} %all-reduce.2.cloned.1.call-done) | copy-start | bytes 786436
  303.9 1.6 copy-start.1
Sparse Core Ops, SparseCore 0:
  18.7 266.9 all-reduce.1
where the time goes:
time: 460 us; the launch traced here: 459 us
  waiting for transfers between devices  271 us (59%)
  blocking collectives  140 us (30%)
  matrix products  21.6 us (5%)
  between operations  16.4 us (4%)
  other arithmetic  6.39 us (1%)
    psum x1, waiting for transfers between devices, local(): gram = lax.psum(local_gram, 'space')  267 us
    psum x1, blocking collectives, local(): squares = lax.psum(jnp.sum(merged * merged, axis=0), 'space')  140 us
  transfers between devices with their start and end apart: 2, of which 2 were waited for; matrix products, arithmetic and copies ran while one was open for 0% of the time, Pallas kernels for 0%

commit v1 on v0

v1 whole, which is shorter than its diff:
```python
import jax
import jax.numpy as jnp
from jax import lax
from jax.experimental import pallas as pl
from jax.experimental.pallas import tpu as pltpu
from jax.sharding import Mesh, PartitionSpec as P

ITERS = 3
NS_STEPS = 6
GRAM_BLOCK = 1024


def gram_kernel(core_ref, own_ref, other_ref, out_ref, acc_ref):
    step = pl.program_id(0)
    stacked = jnp.concatenate([own_ref[...], other_ref[...]], axis=1)
    part = lax.dot_general(
        stacked, stacked, (((0,), (0,)), ((), ())), preferred_element_type=jnp.float32
    )

    @pl.when(step == 0)
    def _():
        acc_ref[...] = part

    @pl.when(step > 0)
    def _():
        acc_ref[...] += part

    last = step == pl.num_programs(0) - 1
    w = own_ref.shape[1]

    @pl.when(last & (core_ref[0] == 0))
    def _():
        out_ref[0:w] = acc_ref[:w, :w]
        out_ref[w : 2 * w] = acc_ref[:w, w:]
        out_ref[2 * w :] = acc_ref[w:, w:]

    @pl.when(last & (core_ref[0] == 1))
    def _():
        out_ref[0:w] = acc_ref[w:, w:]
        out_ref[w : 2 * w] = acc_ref[w:, :w]
        out_ref[2 * w :] = acc_ref[:w, :w]


def half_gram(own, other, core):
    rows, w = own.shape
    steps = rows // 2 // GRAM_BLOCK
    spec = pl.BlockSpec((GRAM_BLOCK, w), lambda i, core_ref: (core_ref[0] * steps + i, 0))
    return pl.pallas_call(
        gram_kernel,
        grid_spec=pltpu.PrefetchScalarGridSpec(
            num_scalar_prefetch=1,
            grid=(steps,),
            in_specs=[spec, spec],
            out_specs=pl.BlockSpec((3 * w, w), lambda i, core_ref: (0, 0)),
            scratch_shapes=[pltpu.VMEM((2 * w, 2 * w), jnp.float32)],
        ),
        out_shape=jax.ShapeDtypeStruct((3 * w, w), jnp.float32),
        compiler_params=pltpu.CompilerParams(vmem_limit_bytes=16 << 20),
    )(core, own, other)


def sum_over_chips(part):
    rows, w = part.shape
    near = ("core", "x")
    n = lax.axis_size("core") * lax.axis_size("x")
    part = lax.all_to_all(part.reshape(n, rows // n, w), near, 0, 0)
    part = jnp.sum(part, axis=0).astype(jnp.bfloat16)
    far = lax.axis_size("z")
    part = lax.all_to_all(jnp.broadcast_to(part[None], (far, rows // n, w)), "z", 0, 0)
    part = jnp.sum(part.astype(jnp.float32), axis=0)
    part = lax.all_to_all(jnp.broadcast_to(part[None], (n, rows // n, w)), near, 0, 0)
    return part.reshape(rows, w)


def polar_iterate(gram, width):
    eye = jnp.eye(width, dtype=jnp.float32)
    start = jnp.concatenate([eye, eye], axis=0) / jnp.sqrt(jnp.float32(2.0))
    for outer in range(ITERS):
        y = jnp.dot(gram, start, precision=lax.Precision.HIGHEST)
        y = y / jnp.sqrt(jnp.sum(y * y) + 1e-06)
        for inner in range(NS_STEPS):
            inner_prod = jnp.dot(y.T, y, precision=lax.Precision.HIGHEST)
            y = 1.5 * y - 0.5 * jnp.dot(y, inner_prod, precision=lax.Precision.HIGHEST)
        start = y
    return start


def local(bases, sing_values):
    width = bases.shape[2]
    rows = bases.shape[1]
    points_all = rows * lax.axis_size("z") * lax.axis_size("x")
    core = lax.axis_index("core")
    own = (bases[0].astype(jnp.float32) * sing_values[0][None, :]).astype(jnp.bfloat16)
    other = lax.ppermute(own, "core", [(0, 1), (1, 0)])
    blocks = sum_over_chips(half_gram(own, other, core.astype(jnp.int32)[None]))
    aa, ab, bb = blocks[:width], blocks[width : 2 * width], blocks[2 * width :]
    gram = jnp.concatenate(
        [jnp.concatenate([aa, ab], axis=1), jnp.concatenate([ab.T, bb], axis=1)], axis=0
    )
    rotation = polar_iterate(gram, width).astype(jnp.bfloat16)
    wide = rotation.astype(jnp.float32)
    squares = jnp.sum(wide * jnp.dot(gram, wide, precision=lax.Precision.HIGHEST), axis=0)
    values = jnp.sqrt(jnp.maximum(squares, 0.0) / points_all + 1e-06)
    first, second = rotation[:width], rotation[width:]
    mine = jnp.where(core == 0, first, second)
    theirs = jnp.where(core == 0, second, first)
    merged = jnp.dot(own, mine, preferred_element_type=jnp.float32)
    merged = merged + jnp.dot(other, theirs, preferred_element_type=jnp.float32)
    merged_bases = (merged / values[None, :]).astype(jnp.bfloat16)
    return (merged_bases[None], values[None])


def solution(mesh):
    fine = Mesh(mesh.devices.reshape(-1, 2, 16, 4), ("y", "core", "z", "x"))
    specs = (P(("y", "core"), ("z", "x"), None), P(("y", "core"), None))
    return jax.shard_map(local, mesh=fine, in_specs=specs, out_specs=specs, check_vma=False)
```

time: 460 us -> 87.4 us (0.19)
  the two profiles are of different devices: /device:TPU:8 before, /device:TPU:1 now
where the time goes in v1:
time: 87.4 us; the launch traced here: 87 us
  blocking collectives  32.6 us (37%)
  matrix products  19.3 us (22%)
  starting transfers between devices  15.8 us (18%)
  waiting for transfers between devices  9.76 us (11%)
  Pallas kernels  3.13 us (4%)
  between operations  2.99 us (3%)
  other arithmetic  2.6 us (3%)
    all_to_all x1, blocking collectives, sum_over_chips(): lax.all_to_all(jnp.broadcast_to(part[None], (far, rows // n, w)), 'z', 0, 0)  23.9 us
    ppermute x1, starting transfers between devices, local(): other = lax.ppermute(own, 'core', [(0, 1), (1, 0)])  8.79 us
    all_to_all x1, blocking collectives, sum_over_chips(): part = lax.all_to_all(part.reshape(n, rows // n, w), near, 0, 0)  8.65 us
    all_to_all x1, starting transfers between devices, sum_over_chips(): lax.all_to_all(jnp.broadcast_to(part[None], (n, rows // n, w)), near, 0, 0)  7.03 us
    dot_general x18, matrix products, polar_iterate(): inner_prod = jnp.dot(y.T, y, precision=lax.Precision.HIGHEST)  6.96 us
    all_to_all x1, waiting for transfers between devices, sum_over_chips(): lax.all_to_all(jnp.broadcast_to(part[None], (n, rows // n, w)), near, 0, 0)  5.87 us
    dot_general x18, matrix products, polar_iterate(): y = 1.5 * y - 0.5 * jnp.dot(y, inner_prod, precision=lax.Precision.HIGHEST)  4.73 us
    ppermute x1, waiting for transfers between devices, local(): other = lax.ppermute(own, 'core', [(0, 1), (1, 0)])  3.89 us
  transfers between devices with their start and end apart: 2, of which 2 were waited for; matrix products, arithmetic and copies ran while one was open for 0% of the time, Pallas kernels for 0%

profile of v1, /device:TPU:1, one launch (start us, length us, event | category | flops | bytes accessed | tf_op | source)
XLA Modules:
  0.0 87.0 jit_solution(9444855911420043866)
XLA Ops:
  0.6 2.0 %fusion.3.own_ref = bf16[8192,128]{1,0:T(8,128)(2,1)S(1)} fusion(bf16[1,8192,128]{2,1,0:T(8,128)(2,1)} %param.2, f32[128]{0:T(128)} %bitcast.83), kind=kLoop, calls=%fused_computation.5 | loop fusion | flops 3145728 | bytes 4194816 | tf_op jit(solution)/shard_map/convert_element_type | solution.py:93
  2.6 8.8 %collective-permute-start = (bf16[8192,128]{1,0:T(8,128)(2,1)S(1)}, bf16[8192,128]{1,0:T(8,128)(2,1)}, u32[]{:S(2)}, u32[]{:S(2)}) collective-permute-start(bf16[8192,128]{1,0:T(8,128)(2,1)S(1)} %fusion.3.own_ref), channel_id=1, source_target_pairs={{0,64},{64,0},{1,65},{65,1},{2,66},{66,2},{3,67},{67,3},{4,68},{68... | collective-permute-start | bytes 6291464 | tf_op jit(solution)/shard_map/ppermute | solution.py:94
  11.4 3.9 %collective-permute-done.other_ref = bf16[8192,128]{1,0:T(8,128)(2,1)} collective-permute-done((bf16[8192,128]{1,0:T(8,128)(2,1)S(1)}, bf16[8192,128]{1,0:T(8,128)(2,1)}, u32[]{:S(2)}, u32[]{:S(2)}) %collective-permute-start) | collective-permute-done | bytes 2097184 | tf_op jit(solution)/shard_map/ppermute | solution.py:94
  15.3 3.1 %shard_map.41 = f32[384,128]{1,0:T(8,128)S(1)} custom-call(s32[1]{0:T(128)} %bitcast.2.core_ref, bf16[8192,128]{1,0:T(8,128)(2,1)S(1)} %fusion.3.own_ref, bf16[8192,128]{1,0:T(8,128)(2,1)} %collective-permute-done.other_ref), custom_call_target="tpu_custom_call" | custom-call | tf_op jit(solution)/shard_map/pallas_call | solution.py:48
  18.5 8.7 %all_to_all.15 = f32[8,48,128]{2,1,0:T(8,128)S(1)} all-to-all(f32[8,48,128]{2,1,0:T(8,128)S(1)} %bitcast.81), channel_id=1, replica_groups=mesh['y'=4,'core'=2,'z'=16,'x'=4] {'core','x'}, dimensions={0} | all-to-all | bytes 393216 | tf_op jit(solution)/shard_map/all_to_all | solution.py:66
  27.2 23.9 %all_to_all.16 = bf16[16,48,128]{2,1,0:T(8,128)(2,1)S(1)} all-to-all(bf16[16,48,128]{2,1,0:T(8,128)(2,1)S(1)} %broadcast_in_dim.9), channel_id=1, replica_groups=mesh['y'=4,'core'=2,'z'=16,'x'=4] {'z'}, dimensions={0} | all-to-all | bytes 393216 | tf_op jit(solution)/shard_map/all_to_all | solution.py:69
  51.1 0.7 broadcast_in_dim.10
  51.8 7.0 %all-to-all-start.2 = ((f32[8,48,128]{2,1,0:T(8,128)}), f32[8,48,128]{2,1,0:T(8,128)S(1)}, u32[]{:S(2)}, u32[]{:S(2)}) async-start(f32[8,48,128]{2,1,0:T(8,128)} %broadcast_in_dim.10), calls=%async_computation.2 | async-start | bytes 393216 | tf_op jit(solution)/shard_map/all_to_all | solution.py:71
  58.8 5.9 %all-to-all-done.2 = f32[8,48,128]{2,1,0:T(8,128)S(1)} async-done(((f32[8,48,128]{2,1,0:T(8,128)}), f32[8,48,128]{2,1,0:T(8,128)S(1)}, u32[]{:S(2)}, u32[]{:S(2)}) %all-to-all-start.2) | async-done | bytes 196640 | tf_op jit(solution)/shard_map/all_to_all | solution.py:71
  64.7 0.1 copy.5
  64.8 1.0 %multiply_reduce_fusion.2 = (f32[]{:T(128)}, f32[256,128]{1,0:T(8,128)S(1)}) fusion(pred[128,128]{1,0:T(32,128)(4,1)S(1)} %iota_compare_fusion, f32[128,128]{1,0:T(8,128)S(1)} %get-tuple-element.4, f32[128,128]{1,0:T(8,128)S(1)} %copy.5, f32[128,128]{1,0:T(8,128)S(1)} %get-tuple-element.5, f32[128,128]{1,0:T(8,128)S(1)} %get-tuple-element.2), kind=kOutput, calls=%fused_computation.49 | convolution fusion | flops 100990976 | bytes 409604 | tf_op jit(solution)/shard_map/dot_general | solution.py:79
  66.5 0.4 fusion.31
  66.9 0.3 fusion.4
  67.2 0.4 fusion.49
  67.6 0.3 fusion.5
  67.8 0.4 fusion.50
  68.2 0.3 fusion.6
  68.5 0.4 fusion.51
  68.9 0.3 fusion.7
  69.2 0.4 fusion.52
  69.6 0.3 fusion.8
  69.8 0.4 fusion.53
  70.2 0.3 fusion.9
  70.5 1.0 %multiply_reduce_fusion.1 = (f32[]{:T(128)}, f32[256,128]{1,0:T(8,128)S(1)}) fusion(f32[256,128]{1,0:T(8,128)S(1)} %fusion.9, f32[128,128]{1,0:T(8,128)S(1)} %get-tuple-element.4, f32[128,128]{1,0:T(8,128)S(1)} %copy.5, f32[128,128]{1,0:T(8,128)S(1)} %get-tuple-element.5, f32[128,128]{1,0:T(8,128)S(1)} %get-tuple-element.2), kind=kOutput, calls=%fused_computation.48 | convolution fusion | flops 100925440 | bytes 524292 | tf_op jit(solution)/shard_map/dot_general | solution.py:79
  72.2 0.4 fusion.32
  72.6 0.3 fusion.10
  72.8 0.4 fusion.54
  73.2 0.3 fusion.11
  73.5 0.4 fusion.55
  73.9 0.3 fusion.12
  74.2 0.4 fusion.56
  74.5 0.3 fusion.13
  74.8 0.4 fusion.57
  75.2 0.3 fusion.14
  75.5 0.4 fusion.58
  75.9 0.3 fusion.15
  76.1 1.0 %multiply_reduce_fusion = (f32[]{:T(128)}, f32[256,128]{1,0:T(8,128)S(1)}) fusion(f32[256,128]{1,0:T(8,128)S(1)} %fusion.15, f32[128,128]{1,0:T(8,128)S(1)} %get-tuple-element.4, f32[128,128]{1,0:T(8,128)S(1)} %copy.5, f32[128,128]{1,0:T(8,128)S(1)} %get-tuple-element.5, f32[128,128]{1,0:T(8,128)S(1)} %get-tuple-element.2), kind=kOutput, calls=%fused_computation.47 | convolution fusion | flops 100925440 | bytes 524292 | tf_op jit(solution)/shard_map/dot_general | solution.py:79
  77.8 0.4 fusion.33
  78.2 0.3 fusion.16
  78.5 0.4 fusion.59
  78.9 0.3 fusion.17
  79.1 0.4 fusion.60
  79.5 0.3 fusion.18
  79.8 0.4 fusion.61
  80.2 0.3 fusion.19
  80.5 0.4 fusion.62
  80.8 0.3 fusion.20
  81.1 0.4 fusion.63
  81.5 0.3 fusion.22
  81.8 0.3 fusion.23
  82.1 0.5 fusion.132
  82.6 0.7 fusion.35
  83.3 3.6 %fusion.2 = bf16[1,8192,128]{2,1,0:T(8,128)(2,1)} fusion(f32[8192,128]{1,0:T(8,128)S(1)} %fusion.35, bf16[8192,128]{1,0:T(8,128)(2,1)} %collective-permute-done.other_ref, f32[128]{0:T(128)S(1)} %add_sqrt_fusion, pred[]{:T(512)S(6)} %eq.9, bf16[256,128]{1,0:T(8,128)(2,1)S(1)} %fusion.22), kind=kOutput, calls=%fused_computation.3 | convolution fusion | flops 271597568 | bytes 8454657 | tf_op jit(solution)/shard_map/dot_general | solution.py:108
  (6 shorter events, 0.1 us)
Async XLA Ops:
  2.6 12.7 %collective-permute-start = (bf16[8192,128]{1,0:T(8,128)(2,1)S(1)}, bf16[8192,128]{1,0:T(8,128)(2,1)}, u32[]{:S(2)}, u32[]{:S(2)}) collective-permute-start(bf16[8192,128]{1,0:T(8,128)(2,1)S(1)} %fusion.3.own_ref), channel_id=1, source_target_pairs={{0,64},{64,0},{1,65},{65,1},{2,66},{66,2},{3,67},{67,3},{4,68},{68... | collective-permute-start | bytes 6291464 | tf_op jit(solution)/shard_map/ppermute | solution.py:94
  51.8 12.9 %all-to-all-start.2 = ((f32[8,48,128]{2,1,0:T(8,128)}), f32[8,48,128]{2,1,0:T(8,128)S(1)}, u32[]{:S(2)}, u32[]{:S(2)}) async-start(f32[8,48,128]{2,1,0:T(8,128)} %broadcast_in_dim.10), calls=%async_computation.2 | async-start | bytes 393216 | tf_op jit(solution)/shard_map/all_to_all | solution.py:71

commit v2 on v0

v2 whole, which is shorter than its diff:
```python
import functools
import math

import jax
import jax.numpy as jnp
from jax import lax
from jax.experimental import pallas as pl
from jax.experimental.pallas import tpu as pltpu
from jax.sharding import Mesh, PartitionSpec as P

ITERS = 3
NS_STEPS = 6
CHUNK = 1024
ROWS = (((0,), (0,)), ((), ()))
PLAIN = (((1,), (0,)), ((), ()))
COLUMNS = (((1,), (1,)), ((), ()))
bf16 = jnp.bfloat16
f32 = jnp.float32


def dot(a, b, dims=PLAIN):
    return lax.dot_general(a, b, dims, preferred_element_type=f32)


def split(x):
    high = x.astype(bf16)
    return high, (x - high.astype(f32)).astype(bf16)


def wide_dot(a, b, dims=PLAIN):
    axis = 1 if dims is PLAIN else 0
    n = b.shape[axis]
    right = jnp.concatenate(split(b), axis=axis)
    right = jnp.concatenate([right, right], axis=1 - axis)
    both = dot(jnp.concatenate(split(a), axis=1), right, dims)
    return both[:, :n] + both[:, n:]


def polar_iterate(gram):
    w = gram.shape[0] // 2
    diag = lax.broadcasted_iota(jnp.int32, (w, w), 0) == lax.broadcasted_iota(jnp.int32, (w, w), 1)
    yt = (gram[:w] + gram[w:]) * f32(1.0 / math.sqrt(2.0))
    for outer in range(ITERS):
        if outer:
            yt = wide_dot(start, gram)
        scale = 1.0 / (jnp.sum(yt * yt) + 1e-06)
        m = wide_dot(yt, yt, COLUMNS) * scale
        yt = yt * jnp.sqrt(scale)
        square = wide_dot(m, m)
        q = 1.5 * diag.astype(f32) - 0.5 * m
        for inner in range(1, NS_STEPS):
            m = 2.25 * m - 1.5 * square + 0.25 * wide_dot(square, m)
            if inner < NS_STEPS - 1:
                both = wide_dot(jnp.concatenate([m, q], axis=0), m)
                square = both[:w]
                q = 1.5 * q - 0.5 * both[w:]
        u = wide_dot(q, yt)
        start = 1.5 * u - 0.5 * wide_dot(m, u)
    return start


def column_squares(gram, rotation):
    high, rest = split(gram)
    low = (gram - high.astype(f32) - rest.astype(f32)).astype(bf16)
    turned = dot(rotation, high) + (dot(rotation, rest) + dot(rotation, low))
    return jnp.sum((turned * rotation.astype(f32)).T, axis=0, keepdims=True)


def finish_kernel(
    points, core_ref, gram_ref, own_a, own_b, other_a, other_b, out_ref, values_ref, rows_ref, sem
):
    w = gram_ref.shape[1]
    aa, ab, bb = gram_ref[:w], gram_ref[w : 2 * w], gram_ref[2 * w :]
    gram = jnp.concatenate(
        [jnp.concatenate([aa, ab], axis=1), jnp.concatenate([ab.T, bb], axis=1)], axis=0
    )
    rotation = polar_iterate(gram).astype(bf16)
    squares = column_squares(gram, rotation)
    values = jnp.sqrt(jnp.maximum(squares, 0.0) / points + 1e-06)
    values_ref[...] = values
    inverse = 1.0 / values
    core = core_ref[0]
    swapped = jnp.concatenate([rotation[:, w:], rotation[:, :w]], axis=1)
    rotation = jnp.where(core == 0, rotation, swapped)
    half = own_a.shape[0]
    copies = []
    for part, (own, other, first) in enumerate(
        [(own_a, other_a, core * half), (own_b, other_b, (1 - core) * half)]
    ):
        for j in range(half // CHUNK):
            rows = pl.ds(j * CHUNK, CHUNK)
            stacked = jnp.concatenate([own[rows], other[rows]], axis=1)
            k = part * (half // CHUNK) + j
            here = rows_ref.at[pl.ds(k * CHUNK, CHUNK)]
            here[...] = (dot(stacked, rotation, COLUMNS) * inverse).astype(bf16)
            there = out_ref.at[pl.ds(pl.multiple_of(first + j * CHUNK, CHUNK), CHUNK)]
            copies.append(pltpu.make_async_copy(here, there, sem.at[k]))
            copies[-1].start()
    for copy in copies:
        copy.wait()


def finish(core, blocks, own_a, own_b, other_a, other_b, points):
    half, w = own_a.shape
    vmem = pl.BlockSpec(memory_space=pltpu.VMEM)
    return pl.pallas_call(
        functools.partial(finish_kernel, points),
        in_specs=[pl.BlockSpec(memory_space=pltpu.SMEM)] + [vmem] * 5,
        out_specs=[pl.BlockSpec(memory_space=pl.ANY), vmem],
        out_shape=[jax.ShapeDtypeStruct((2 * half, w), bf16), jax.ShapeDtypeStruct((1, w), f32)],
        scratch_shapes=[
            pltpu.VMEM((2 * half, w), bf16),
            pltpu.SemaphoreType.DMA((2 * half // CHUNK,)),
        ],
        compiler_params=pltpu.CompilerParams(vmem_limit_bytes=24 << 20),
    )(core, blocks, own_a, own_b, other_a, other_b)


def gram_kernel(core_ref, own_ref, other_ref, out_ref):
    w = own_ref.shape[1]
    stacked = jnp.concatenate([own_ref[...], other_ref[...]], axis=1)
    gram = dot(stacked, stacked, ROWS)

    @pl.when(core_ref[0] == 0)
    def _():
        out_ref[0:w] = gram[:w, :w]
        out_ref[w : 2 * w] = gram[:w, w:]
        out_ref[2 * w :] = gram[w:, w:]

    @pl.when(core_ref[0] != 0)
    def _():
        out_ref[0:w] = gram[w:, w:]
        out_ref[w : 2 * w] = gram[w:, :w]
        out_ref[2 * w :] = gram[:w, :w]


def half_gram(core, own, other):
    w = own.shape[1]
    vmem = pl.BlockSpec(memory_space=pltpu.VMEM)
    return pl.pallas_call(
        gram_kernel,
        in_specs=[pl.BlockSpec(memory_space=pltpu.SMEM), vmem, vmem],
        out_specs=vmem,
        out_shape=jax.ShapeDtypeStruct((3 * w, w), f32),
        compiler_params=pltpu.CompilerParams(vmem_limit_bytes=24 << 20),
    )(core, own, other)


def sum_over_chips(part):
    rows, w = part.shape
    near = ("core", "x")
    n = lax.axis_size("core") * lax.axis_size("x")
    part = lax.all_to_all(part.reshape(n, rows // n, w), near, 0, 0)
    part = jnp.sum(part, axis=0).astype(bf16)
    far = lax.axis_size("z")
    part = lax.all_to_all(jnp.broadcast_to(part[None], (far, rows // n, w)), "z", 0, 0)
    part = jnp.sum(part.astype(f32), axis=0)
    part = lax.all_to_all(jnp.broadcast_to(part[None], (n, rows // n, w)), near, 0, 0)
    return part.reshape(rows, w)


def local(bases, sing_values):
    rows = bases.shape[1]
    half = rows // 2
    points = rows * lax.axis_size("z") * lax.axis_size("x")
    core = lax.axis_index("core").astype(jnp.int32)

    def weighted(first):
        part = lax.dynamic_slice_in_dim(bases[0], first, half)
        return (part.astype(f32) * sing_values[0][None, :]).astype(bf16)

    def partners(value):
        return lax.ppermute(value, "core", [(0, 1), (1, 0)])

    own_b = weighted((1 - core) * half)
    other_a = partners(own_b)
    own_a = weighted(core * half)
    other_b = partners(own_a)
    blocks = sum_over_chips(half_gram(core[None], own_a, other_a))
    merged, values = finish(core[None], blocks, own_a, own_b, other_a, other_b, points)
    return (merged[None], values)


def solution(mesh):
    fine = Mesh(mesh.devices.reshape(-1, 2, 16, 4), ("y", "core", "z", "x"))
    specs = (P(("y", "core"), ("z", "x"), None), P(("y", "core"), None))
    return jax.shard_map(local, mesh=fine, in_specs=specs, out_specs=specs, check_vma=False)
```

time: 460 us -> 72.5 us (0.16)
  the two profiles are of different devices: /device:TPU:8 before, /device:TPU:1 now
where the time goes in v2:
time: 72.5 us; the launch traced here: 72.1 us
  blocking collectives  23.2 us (32%)
  starting transfers between devices  21.5 us (30%)
  waiting for transfers between devices  12 us (17%)
  Pallas kernels  12 us (17%)
  other arithmetic  2.01 us (3%)
    all_to_all x1, blocking collectives, sum_over_chips(): lax.all_to_all(jnp.broadcast_to(part[None], (far, rows // n, w)), 'z', 0, 0)  23.2 us
    ppermute x2, starting transfers between devices, partners(): return lax.ppermute(value, 'core', [(0, 1), (1, 0)])  10.8 us
    pallas_call x1, Pallas kernels, finish(): pl.pallas_call(functools.partial(finish_kernel, points), in_specs=[pl.Blo...  10.5 us
    all_to_all x1, starting transfers between devices, sum_over_chips(): lax.all_to_all(jnp.broadcast_to(part[None], (n, rows // n, w)), near, 0, 0)  7.03 us
    all_to_all x1, waiting for transfers between devices, sum_over_chips(): lax.all_to_all(jnp.broadcast_to(part[None], (n, rows // n, w)), near, 0, 0)  5.89 us
    all_to_all x1, waiting for transfers between devices, sum_over_chips(): part = lax.all_to_all(part.reshape(n, rows // n, w), near, 0, 0)  3.89 us
    all_to_all x1, starting transfers between devices, sum_over_chips(): part = lax.all_to_all(part.reshape(n, rows // n, w), near, 0, 0)  3.68 us
    ppermute x2, waiting for transfers between devices, partners(): return lax.ppermute(value, 'core', [(0, 1), (1, 0)])  2.27 us
  transfers between devices with their start and end apart: 4, of which 3 were waited for; matrix products, arithmetic and copies ran while one was open for 1% of the time, Pallas kernels for 0%

profile of v2, /device:TPU:1, one launch (start us, length us, event | category | flops | bytes accessed | tf_op | source)
XLA Modules:
  0.0 72.1 jit_solution(8679938256303071035)
XLA Ops:
  0.6 2.0 %fusion = (bf16[4096,128]{1,0:T(8,128)(2,1)S(1)}, bf16[4096,128]{1,0:T(8,128)(2,1)S(1)}) fusion(bf16[1,8192,128]{2,1,0:T(8,128)(2,1)} %param.2, s32[]{:T(128)S(6)} %select_n.7, f32[128]{0:T(128)} %bitcast.12, s32[]{:T(128)S(6)} %select_n.6), kind=kLoop, calls=%fused_computation.1 | loop fusion | flops 3145728 | bytes 4194824 | tf_op jit(solution)/shard_map/convert_element_type | solution.py:170
  2.6 8.8 %collective-permute-start = (bf16[4096,128]{1,0:T(8,128)(2,1)S(1)}, bf16[4096,128]{1,0:T(8,128)(2,1)S(1)}, u32[]{:S(2)}, u32[]{:S(2)}) collective-permute-start(bf16[4096,128]{1,0:T(8,128)(2,1)S(1)} %get-tuple-element.6.own_b), channel_id=1, source_target_pairs={{0,64},{64,0},{1,65},{65,1},{2,66},{66,2},{3,67},{67,3},{4,68},{68... | collective-permute-start | bytes 3145736 | tf_op jit(solution)/shard_map/ppermute | solution.py:173
  11.4 2.3 %collective-permute-done.other_ref.other_a = bf16[4096,128]{1,0:T(8,128)(2,1)S(1)} collective-permute-done((bf16[4096,128]{1,0:T(8,128)(2,1)S(1)}, bf16[4096,128]{1,0:T(8,128)(2,1)S(1)}, u32[]{:S(2)}, u32[]{:S(2)}) %collective-permute-start) | collective-permute-done | bytes 1048608 | tf_op jit(solution)/shard_map/ppermute | solution.py:173
  13.7 1.4 %shard_map.41 = f32[384,128]{1,0:T(8,128)} custom-call(s32[1]{0:T(128)} %bitcast.core_ref, bf16[4096,128]{1,0:T(8,128)(2,1)S(1)} %get-tuple-element.7.own_ref.own_a, bf16[4096,128]{1,0:T(8,128)(2,1)S(1)} %collective-permute-done.other_ref.other_a), custom_call_target="tpu_custom_call" | custom-call | tf_op jit(solution)/shard_map/pallas_call | solution.py:140
  15.1 3.7 %all-to-all-start = ((f32[8,48,128]{2,1,0:T(8,128)}), f32[8,48,128]{2,1,0:T(8,128)S(1)}, u32[]{:S(2)}, u32[]{:S(2)}) async-start(f32[8,48,128]{2,1,0:T(8,128)} %bitcast.4), calls=%async_computation | async-start | bytes 393216 | tf_op jit(solution)/shard_map/all_to_all | solution.py:153
  18.8 2.0 %collective-permute-start.1 = (bf16[4096,128]{1,0:T(8,128)(2,1)S(1)}, bf16[4096,128]{1,0:T(8,128)(2,1)}, u32[]{:S(2)}, u32[]{:S(2)}) collective-permute-start(bf16[4096,128]{1,0:T(8,128)(2,1)S(1)} %get-tuple-element.7.own_ref.own_a), channel_id=1, source_target_pairs={{0,64},{64,0},{1,65},{65,1},{2,66},{66,2},{3,67},{67,3},{4,68},{68... | collective-permute-start | bytes 3145736 | tf_op jit(solution)/shard_map/ppermute | solution.py:173
  20.8 3.9 %all-to-all-done = f32[8,48,128]{2,1,0:T(8,128)S(1)} async-done(((f32[8,48,128]{2,1,0:T(8,128)}), f32[8,48,128]{2,1,0:T(8,128)S(1)}, u32[]{:S(2)}, u32[]{:S(2)}) %all-to-all-start) | async-done | bytes 196640 | tf_op jit(solution)/shard_map/all_to_all | solution.py:153
  24.7 23.2 %all_to_all.15 = bf16[16,48,128]{2,1,0:T(8,128)(2,1)S(1)} all-to-all(bf16[16,48,128]{2,1,0:T(8,128)(2,1)S(1)} %broadcast_in_dim.9), channel_id=1, replica_groups=mesh['y'=4,'core'=2,'z'=16,'x'=4] {'z'}, dimensions={0} | all-to-all | bytes 393216 | tf_op jit(solution)/shard_map/all_to_all | solution.py:156
  47.9 0.7 broadcast_in_dim.10
  48.6 7.0 %all-to-all-start.2 = ((f32[8,48,128]{2,1,0:T(8,128)}), f32[8,48,128]{2,1,0:T(8,128)S(1)}, u32[]{:S(2)}, u32[]{:S(2)}) async-start(f32[8,48,128]{2,1,0:T(8,128)} %broadcast_in_dim.10), calls=%async_computation.2 | async-start | bytes 393216 | tf_op jit(solution)/shard_map/all_to_all | solution.py:158
  55.7 0.0 collective-permute-done.1.other_b
  55.7 5.9 %all-to-all-done.2 = f32[8,48,128]{2,1,0:T(8,128)S(1)} async-done(((f32[8,48,128]{2,1,0:T(8,128)}), f32[8,48,128]{2,1,0:T(8,128)S(1)}, u32[]{:S(2)}, u32[]{:S(2)}) %all-to-all-start.2) | async-done | bytes 196640 | tf_op jit(solution)/shard_map/all_to_all | solution.py:158
  61.6 10.5 %shard_map.42 = (bf16[8192,128]{1,0:T(8,128)(2,1)}, f32[1,128]{1,0:T(1,128)}) custom-call(s32[1]{0:T(128)} %bitcast.core_ref, f32[384,128]{1,0:T(8,128)S(1)} %bitcast.11, bf16[4096,128]{1,0:T(8,128)(2,1)S(1)} %get-tuple-element.7.own_ref.own_a, bf16[4096,128]{1,0:T(8,128)(2,1)S(1)} %get-tuple-element.6.own_b, ...), custom_call_target="tpu_custom_call" | custom-call | tf_op jit(solution)/shard_map/pallas_call | solution.py:106
  (3 shorter events, 0.1 us)
Async XLA Ops:
  2.6 11.1 %collective-permute-start = (bf16[4096,128]{1,0:T(8,128)(2,1)S(1)}, bf16[4096,128]{1,0:T(8,128)(2,1)S(1)}, u32[]{:S(2)}, u32[]{:S(2)}) collective-permute-start(bf16[4096,128]{1,0:T(8,128)(2,1)S(1)} %get-tuple-element.6.own_b), channel_id=1, source_target_pairs={{0,64},{64,0},{1,65},{65,1},{2,66},{66,2},{3,67},{67,3},{4,68},{68... | collective-permute-start | bytes 3145736 | tf_op jit(solution)/shard_map/ppermute | solution.py:173
  15.1 9.6 %all-to-all-start = ((f32[8,48,128]{2,1,0:T(8,128)}), f32[8,48,128]{2,1,0:T(8,128)S(1)}, u32[]{:S(2)}, u32[]{:S(2)}) async-start(f32[8,48,128]{2,1,0:T(8,128)} %bitcast.4), calls=%async_computation | async-start | bytes 393216 | tf_op jit(solution)/shard_map/all_to_all | solution.py:153
  18.8 36.9 %collective-permute-start.1 = (bf16[4096,128]{1,0:T(8,128)(2,1)S(1)}, bf16[4096,128]{1,0:T(8,128)(2,1)}, u32[]{:S(2)}, u32[]{:S(2)}) collective-permute-start(bf16[4096,128]{1,0:T(8,128)(2,1)S(1)} %get-tuple-element.7.own_ref.own_a), channel_id=1, source_target_pairs={{0,64},{64,0},{1,65},{65,1},{2,66},{66,2},{3,67},{67,3},{4,68},{68... | collective-permute-start | bytes 3145736 | tf_op jit(solution)/shard_map/ppermute | solution.py:173
  48.6 12.9 %all-to-all-start.2 = ((f32[8,48,128]{2,1,0:T(8,128)}), f32[8,48,128]{2,1,0:T(8,128)S(1)}, u32[]{:S(2)}, u32[]{:S(2)}) async-start(f32[8,48,128]{2,1,0:T(8,128)} %broadcast_in_dim.10), calls=%async_computation.2 | async-start | bytes 393216 | tf_op jit(solution)/shard_map/all_to_all | solution.py:158

commit v3 on v2

--- a/solution.py
+++ b/solution.py
@@ -67,9 +67,21 @@
 
 
 def finish_kernel(
-    points, core_ref, gram_ref, own_a, own_b, other_a, other_b, out_ref, values_ref, rows_ref, sem
+    points, core_ref, gram_ref, weights_hbm, bases_ref, near_ref, far_ref,
+    out_ref, values_ref, weights_ref, own_ref, other_ref, rows_ref, sem, out_sem,
 ):
-    w = gram_ref.shape[1]
+    core = core_ref[0]
+    rows, w = own_ref.shape
+    half = rows // 2
+    here, there = (pl.ds(pl.multiple_of(c * half, half), half) for c in (core, 1 - core))
+    loads = [
+        pltpu.make_async_copy(bases_ref, own_ref, sem.at[0]),
+        pltpu.make_async_copy(near_ref, other_ref.at[here], sem.at[1]),
+        pltpu.make_async_copy(far_ref, other_ref.at[there], sem.at[2]),
+        pltpu.make_async_copy(weights_hbm, weights_ref, sem.at[3]),
+    ]
+    for load in loads:
+        load.start()
     aa, ab, bb = gram_ref[:w], gram_ref[w : 2 * w], gram_ref[2 * w :]
     gram = jnp.concatenate(
         [jnp.concatenate([aa, ab], axis=1), jnp.concatenate([ab.T, bb], axis=1)], axis=0
@@ -79,41 +91,79 @@
     values = jnp.sqrt(jnp.maximum(squares, 0.0) / points + 1e-06)
     values_ref[...] = values
     inverse = 1.0 / values
-    core = core_ref[0]
     swapped = jnp.concatenate([rotation[:, w:], rotation[:, :w]], axis=1)
     rotation = jnp.where(core == 0, rotation, swapped)
-    half = own_a.shape[0]
+    for load in loads:
+        load.wait()
     copies = []
-    for part, (own, other, first) in enumerate(
-        [(own_a, other_a, core * half), (own_b, other_b, (1 - core) * half)]
-    ):
-        for j in range(half // CHUNK):
-            rows = pl.ds(j * CHUNK, CHUNK)
-            stacked = jnp.concatenate([own[rows], other[rows]], axis=1)
-            k = part * (half // CHUNK) + j
-            here = rows_ref.at[pl.ds(k * CHUNK, CHUNK)]
-            here[...] = (dot(stacked, rotation, COLUMNS) * inverse).astype(bf16)
-            there = out_ref.at[pl.ds(pl.multiple_of(first + j * CHUNK, CHUNK), CHUNK)]
-            copies.append(pltpu.make_async_copy(here, there, sem.at[k]))
-            copies[-1].start()
+    for j in range(rows // CHUNK):
+        part = pl.ds(j * CHUNK, CHUNK)
+        own = (own_ref[part].astype(f32) * weights_ref[...]).astype(bf16)
+        stacked = jnp.concatenate([own, other_ref[part]], axis=1)
+        rows_ref[part] = (dot(stacked, rotation, COLUMNS) * inverse).astype(bf16)
+        copies.append(pltpu.make_async_copy(rows_ref.at[part], out_ref.at[part], out_sem.at[j]))
+        copies[-1].start()
     for copy in copies:
         copy.wait()
 
 
-def finish(core, blocks, own_a, own_b, other_a, other_b, points):
-    half, w = own_a.shape
-    vmem = pl.BlockSpec(memory_space=pltpu.VMEM)
+def finish(core, blocks, sing_values, bases, near, far, points):
+    rows, w = bases.shape
+    vmem = pl.BlockSpec(memory_space=pltpu.VMEM)
+    anywhere = pl.BlockSpec(memory_space=pl.ANY)
     return pl.pallas_call(
         functools.partial(finish_kernel, points),
-        in_specs=[pl.BlockSpec(memory_space=pltpu.SMEM)] + [vmem] * 5,
-        out_specs=[pl.BlockSpec(memory_space=pl.ANY), vmem],
-        out_shape=[jax.ShapeDtypeStruct((2 * half, w), bf16), jax.ShapeDtypeStruct((1, w), f32)],
+        in_specs=[pl.BlockSpec(memory_space=pltpu.SMEM), vmem]
+        + [pl.BlockSpec(memory_space=pltpu.HBM)] * 2
+        + [anywhere] * 2,
+        out_specs=[anywhere, vmem],
+        out_shape=[jax.ShapeDtypeStruct((rows, w), bf16), jax.ShapeDtypeStruct((1, w), f32)],
         scratch_shapes=[
-            pltpu.VMEM((2 * half, w), bf16),
-            pltpu.SemaphoreType.DMA((2 * half // CHUNK,)),
+            pltpu.VMEM(sing_values.shape, f32),
+            pltpu.VMEM((rows, w), bf16),
+            pltpu.VMEM((rows, w), bf16),
+            pltpu.VMEM((rows, w), bf16),
+            pltpu.SemaphoreType.DMA((4,)),
+            pltpu.SemaphoreType.DMA((rows // CHUNK,)),
         ],
-        compiler_params=pltpu.CompilerParams(vmem_limit_bytes=24 << 20),
-    )(core, blocks, own_a, own_b, other_a, other_b)
+        compiler_params=pltpu.CompilerParams(vmem_limit_bytes=16 << 20),
+    )(core, blocks, sing_values, bases, near, far)
+
+
+def weigh_kernel(block_ref, weights_hbm, bases_ref, out_ref, weights_ref, rows_ref, sem):
+    half = out_ref.shape[0]
+    weights = pltpu.make_async_copy(weights_hbm, weights_ref, sem.at[half // CHUNK])
+    weights.start()
+    copies = []
+    for j in range(half // CHUNK):
+        first = pl.multiple_of(block_ref[0] * half + j * CHUNK, CHUNK)
+        here = rows_ref.at[pl.ds(j * CHUNK, CHUNK)]
+        copies.append(pltpu.make_async_copy(bases_ref.at[pl.ds(first, CHUNK)], here, sem.at[j]))
+        copies[-1].start()
+    weights.wait()
+    for j, copy in enumerate(copies):
+        copy.wait()
+        rows = pl.ds(j * CHUNK, CHUNK)
+        out_ref[rows] = (rows_ref[rows].astype(f32) * weights_ref[...]).astype(bf16)
+
+
+def weigh_half(block, sing_values, bases):
+    rows, w = bases.shape
+    half = rows // 2
+    vmem = pl.BlockSpec(memory_space=pltpu.VMEM)
+    return pl.pallas_call(
+        weigh_kernel,
+        in_specs=[pl.BlockSpec(memory_space=pltpu.SMEM)] + [pl.BlockSpec(memory_space=pltpu.HBM)] * 2,
+        out_specs=vmem,
+        out_shape=pltpu.VMEM((half, w), bf16),
+        scratch_shapes=[
+            pltpu.VMEM(sing_values.shape, f32),
+            pltpu.VMEM((half, w), bf16),
+            pltpu.SemaphoreType.DMA((half // CHUNK + 1,)),
+        ],
+        compiler_params=pltpu.CompilerParams(vmem_limit_bytes=4 << 20),
+        cost_estimate=pl.CostEstimate(flops=half * w, bytes_accessed=4 * half * w, transcendentals=0),
+    )(block, sing_values, bases)
 
 
 def gram_kernel(core_ref, own_ref, other_ref, out_ref):
@@ -142,19 +192,36 @@
         in_specs=[pl.BlockSpec(memory_space=pltpu.SMEM), vmem, vmem],
         out_specs=vmem,
         out_shape=jax.ShapeDtypeStruct((3 * w, w), f32),
-        compiler_params=pltpu.CompilerParams(vmem_limit_bytes=24 << 20),
+        compiler_params=pltpu.CompilerParams(vmem_limit_bytes=12 << 20),
     )(core, own, other)
 
 
-def sum_over_chips(part):
+def add_kernel(after_ref, parts_ref, out_ref):
+    total = jnp.sum(parts_ref[...], axis=0)
+    for k in range(out_ref.shape[0]):
+        out_ref[k] = total
+
+
+def add_and_repeat(parts, repeats, after):
+    vmem = pl.BlockSpec(memory_space=pltpu.VMEM)
+    return pl.pallas_call(
+        add_kernel,
+        in_specs=[pl.BlockSpec(memory_space=pl.ANY), vmem],
+        out_specs=vmem,
+        out_shape=jax.ShapeDtypeStruct((repeats, *parts.shape[1:]), f32),
+        compiler_params=pltpu.CompilerParams(vmem_limit_bytes=2 << 20),
+    )(after, parts)
+
+
+def sum_over_chips(part, after):
     rows, w = part.shape
-    near = ("core", "x")
-    n = lax.axis_size("core") * lax.axis_size("x")
+    near, far = ("core", "z_lo", "x"), "z_hi"
+    n, m = math.prod(lax.axis_size(axis) for axis in near), lax.axis_size(far)
     part = lax.all_to_all(part.reshape(n, rows // n, w), near, 0, 0)
-    part = jnp.sum(part, axis=0).astype(bf16)
-    far = lax.axis_size("z")
-    part = lax.all_to_all(jnp.broadcast_to(part[None], (far, rows // n, w)), "z", 0, 0)
-    part = jnp.sum(part.astype(f32), axis=0)
+    part = add_and_repeat(part, m, after)
+    turned = [[(i + m // 2) % m for i in range(m)]]
+    part = lax.all_to_all(part, far, 0, 0, axis_index_groups=turned)
+    part = jnp.sum(part, axis=0)
     part = lax.all_to_all(jnp.broadcast_to(part[None], (n, rows // n, w)), near, 0, 0)
     return part.reshape(rows, w)
 
@@ -162,26 +229,26 @@
 def local(bases, sing_values):
     rows = bases.shape[1]
     half = rows // 2
-    points = rows * lax.axis_size("z") * lax.axis_size("x")
+    points = rows * math.prod(lax.axis_size(axis) for axis in ("z_hi", "z_lo", "x"))
     core = lax.axis_index("core").astype(jnp.int32)
-
-    def weighted(first):
-        part = lax.dynamic_slice_in_dim(bases[0], first, half)
-        return (part.astype(f32) * sing_values[0][None, :]).astype(bf16)
 
     def partners(value):
         return lax.ppermute(value, "core", [(0, 1), (1, 0)])
 
-    own_b = weighted((1 - core) * half)
+    bases = pltpu.with_memory_space_constraint(bases[0], pltpu.HBM)
+    sing_values = pltpu.with_memory_space_constraint(sing_values, pltpu.HBM)
+    own_b = weigh_half(1 - core[None], sing_values, bases)
     other_a = partners(own_b)
-    own_a = weighted(core * half)
+    own_a = weigh_half(core[None], sing_values, bases)
     other_b = partners(own_a)
-    blocks = sum_over_chips(half_gram(core[None], own_a, other_a))
-    merged, values = finish(core[None], blocks, own_a, own_b, other_a, other_b, points)
+    blocks = sum_over_chips(half_gram(core[None], own_a, other_a), other_b)
+    merged, values = finish(
+        core[None], blocks, sing_values, bases, other_a, other_b, points
+    )
     return (merged[None], values)
 
 
 def solution(mesh):
-    fine = Mesh(mesh.devices.reshape(-1, 2, 16, 4), ("y", "core", "z", "x"))
-    specs = (P(("y", "core"), ("z", "x"), None), P(("y", "core"), None))
+    fine = Mesh(mesh.devices.reshape(-1, 2, 8, 2, 4), ("y", "core", "z_hi", "z_lo", "x"))
+    specs = (P(("y", "core"), ("z_hi", "z_lo", "x"), None), P(("y", "core"), None))
     return jax.shard_map(local, mesh=fine, in_specs=specs, out_specs=specs, check_vma=False)

time: 72.5 us -> 65.8 us (0.908)
  starting transfers between devices: 21.5 us -> 14.6 us
  blocking collectives: 23.2 us -> 29.2 us
  waiting for transfers between devices: 12 us -> 7.05 us
  other arithmetic: 2.01 us -> 0.01 us
  Pallas kernels: 12 us -> 13.9 us
    all_to_all x1 -> x0, starting transfers between devices: 7.03 us -> none  [sum_over_chips(): lax.all_to_all(jnp.broadcast_to(part[None], (n, rows // n, w)), near, 0, 0)]
    all_to_all x1 -> x2, blocking collectives: 23.2 us -> 29.2 us  [the longest x1 18.1 us: sum_over_chips(): part = lax.all_to_all(part, far, 0, 0, axis_index_groups=turned)]
    all_to_all x1 -> x0, waiting for transfers between devices: 5.89 us -> none  [sum_over_chips(): lax.all_to_all(jnp.broadcast_to(part[None], (n, rows // n, w)), near, 0, 0)]
    all_to_all x1, waiting for transfers between devices: 3.89 us -> 7.05 us  [sum_over_chips(): part = lax.all_to_all(part.reshape(n, rows // n, w), near, 0, 0)]
    pallas_call x0 -> x3, Pallas kernels: none -> 2.61 us  [the longest x2 2.59 us: weigh_half(): pl.pallas_call(weigh_kernel, in_specs=[pl.BlockSpec(memory_space=pltpu.SM...]
    ppermute x2, waiting for transfers between devices: 2.27 us -> 0.01 us  [partners(): return lax.ppermute(value, 'core', [(0, 1), (1, 0)])]
    convert_element_type x1 -> x0, other arithmetic: 1.96 us -> none  [weighted(): return (part.astype(f32) * sing_values[0][None, :]).astype(bf16)]
  transfers between devices with their start and end apart: 4 -> 3, of which waited for: 3 -> 1; matrix products, arithmetic and copies ran while one was open for 1% -> 0% of each run, Pallas kernels for 0% -> 4%
where the time goes in v3:
time: 65.8 us; the launch traced here: 65.5 us
  blocking collectives  29.2 us (44%)
  starting transfers between devices  14.6 us (22%)
  Pallas kernels  13.9 us (21%)
  waiting for transfers between devices  7.05 us (11%)
  between operations  0.69 us (1%)
    all_to_all x1, blocking collectives, sum_over_chips(): part = lax.all_to_all(part, far, 0, 0, axis_index_groups=turned)  18.1 us
    all_to_all x1, blocking collectives, sum_over_chips(): lax.all_to_all(jnp.broadcast_to(part[None], (n, rows // n, w)), near, 0, 0)  11.2 us
    ppermute x2, starting transfers between devices, partners(): return lax.ppermute(value, 'core', [(0, 1), (1, 0)])  10.7 us
    pallas_call x1, Pallas kernels, finish(): pl.pallas_call(functools.partial(finish_kernel, points), in_specs=[pl.Blo...  9.84 us
    all_to_all x1, waiting for transfers between devices, sum_over_chips(): part = lax.all_to_all(part.reshape(n, rows // n, w), near, 0, 0)  7.05 us
    all_to_all x1, starting transfers between devices, sum_over_chips(): part = lax.all_to_all(part.reshape(n, rows // n, w), near, 0, 0)  3.85 us
    pallas_call x2, Pallas kernels, weigh_half(): pl.pallas_call(weigh_kernel, in_specs=[pl.BlockSpec(memory_space=pltpu.SM...  2.59 us
    pallas_call x1, Pallas kernels, half_gram(): pl.pallas_call(gram_kernel, in_specs=[pl.BlockSpec(memory_space=pltpu.SME...  1.45 us
  transfers between devices with their start and end apart: 3, of which 1 were waited for; matrix products, arithmetic and copies ran while one was open for 0% of the time, Pallas kernels for 4%

profile of v3, /device:TPU:1, one launch (start us, length us, event | category | flops | bytes accessed | tf_op | source)
XLA Modules:
  0.0 65.5 jit_solution(5181064389582515338)
XLA Ops:
  0.6 1.3 %shard_map.42 = bf16[4096,128]{1,0:T(8,128)(2,1)S(1)} custom-call(s32[1]{0:T(128)S(6)} %sub.3.block_ref, f32[1,128]{1,0:T(1,128)} %weights_hbm.5, bf16[8192,128]{1,0:T(8,128)(2,1)} %bitcast.6), custom_call_target="tpu_custom_call" | custom-call | flops 524288 | bytes 2097152 | tf_op jit(solution)/shard_map/pallas_call | solution.py:154
  1.9 8.8 %collective-permute-start.1 = (bf16[4096,128]{1,0:T(8,128)(2,1)S(1)}, bf16[4096,128]{1,0:T(8,128)(2,1)S(1)}, u32[]{:S(2)}, u32[]{:S(2)}) collective-permute-start(bf16[4096,128]{1,0:T(8,128)(2,1)S(1)} %shard_map.42), channel_id=1, source_target_pairs={{0,64},{64,0},{1,65},{65,1},{2,66},{66,2},{3,67},{67,3},{4,68},{68... | collective-permute-start | bytes 3145736 | tf_op jit(solution)/shard_map/ppermute | solution.py:236
  10.7 1.3 %shard_map.41.own_ref = bf16[4096,128]{1,0:T(8,128)(2,1)S(1)} custom-call(s32[1]{0:T(128)} %bitcast.block_ref.core_ref, f32[1,128]{1,0:T(1,128)} %weights_hbm.5, bf16[8192,128]{1,0:T(8,128)(2,1)} %bitcast.7), custom_call_target="tpu_custom_call" | custom-call | flops 524288 | bytes 2097152 | tf_op jit(solution)/shard_map/pallas_call | solution.py:154
  12.0 1.9 %collective-permute-start = (bf16[4096,128]{1,0:T(8,128)(2,1)S(1)}, bf16[4096,128]{1,0:T(8,128)(2,1)S(1)}, u32[]{:S(2)}, u32[]{:S(2)}) collective-permute-start(bf16[4096,128]{1,0:T(8,128)(2,1)S(1)} %shard_map.41.own_ref), channel_id=1, source_target_pairs={{0,64},{64,0},{1,65},{65,1},{2,66},{66,2},{3,67},{67,3},{4,68},{68... | collective-permute-start | bytes 3145736 | tf_op jit(solution)/shard_map/ppermute | solution.py:236
  14.0 0.0 collective-permute-done.1.other_ref.near_ref
  14.0 1.4 %shard_map.43 = f32[384,128]{1,0:T(8,128)} custom-call(s32[1]{0:T(128)} %bitcast.block_ref.core_ref, bf16[4096,128]{1,0:T(8,128)(2,1)S(1)} %shard_map.41.own_ref, bf16[4096,128]{1,0:T(8,128)(2,1)S(1)} %collective-permute-done.1.other_ref.near_ref), custom_call_target="tpu_custom_call" | custom-call | tf_op jit(solution)/shard_map/pallas_call | solution.py:190
  15.4 3.8 %all-to-all-start = ((f32[16,24,128]{2,1,0:T(8,128)}), f32[16,24,128]{2,1,0:T(8,128)S(1)}, u32[]{:S(2)}, u32[]{:S(2)}) async-start(f32[16,24,128]{2,1,0:T(8,128)} %bitcast.2), calls=%async_computation | async-start | bytes 393216 | tf_op jit(solution)/shard_map/all_to_all | solution.py:220
  19.3 0.0 collective-permute-done.after_ref.far_ref
  19.3 7.0 %all-to-all-done.parts_ref = f32[16,24,128]{2,1,0:T(8,128)S(1)} async-done(((f32[16,24,128]{2,1,0:T(8,128)}), f32[16,24,128]{2,1,0:T(8,128)S(1)}, u32[]{:S(2)}, u32[]{:S(2)}) %all-to-all-start) | async-done | bytes 196640 | tf_op jit(solution)/shard_map/all_to_all | solution.py:220
  26.4 18.1 %all_to_all.15 = f32[8,24,128]{2,1,0:T(8,128)S(1)} all-to-all(f32[8,24,128]{2,1,0:T(8,128)S(1)} %shard_map.44), channel_id=1, replica_groups={{32,40,48,56,0,8,16,24},{33,41,49,57,1,9,17,25},{34,42,50,58,2,10,18,26..., dimensions={0} | all-to-all | bytes 196608 | tf_op jit(solution)/shard_map/all_to_all | solution.py:223
  44.4 11.2 %all_to_all.16 = f32[16,24,128]{2,1,0:T(8,128)S(1)} all-to-all(f32[16,24,128]{2,1,0:T(8,128)S(1)} %broadcast_in_dim.7), channel_id=1, replica_groups=mesh['y'=4,'core'=2,'z_hi'=8,'z_lo'=2,'x'=4] {'core','z_lo','x'}, dimensions={0} | all-to-all | bytes 393216 | tf_op jit(solution)/shard_map/all_to_all | solution.py:225
  55.6 9.8 %shard_map.45 = (bf16[8192,128]{1,0:T(8,128)(2,1)}, f32[1,128]{1,0:T(1,128)}) custom-call(s32[1]{0:T(128)} %bitcast.block_ref.core_ref, f32[384,128]{1,0:T(8,128)S(1)} %bitcast.5, f32[1,128]{1,0:T(1,128)} %weights_hbm.5, bf16[8192,128]{1,0:T(8,128)(2,1)} %bitcast.8, bf16[4096,128]{1,0:T(8,128)(2,1)S(1)} %collective-permute-done.1.other_ref.near_ref, ...), custom_call_target="tpu_custom_call" | custom-call | tf_op jit(solution)/shard_map/pallas_call | solution.py:114
  (3 shorter events, 0.0 us)
Async XLA Ops:
  1.9 12.0 %collective-permute-start.1 = (bf16[4096,128]{1,0:T(8,128)(2,1)S(1)}, bf16[4096,128]{1,0:T(8,128)(2,1)S(1)}, u32[]{:S(2)}, u32[]{:S(2)}) collective-permute-start(bf16[4096,128]{1,0:T(8,128)(2,1)S(1)} %shard_map.42), channel_id=1, source_target_pairs={{0,64},{64,0},{1,65},{65,1},{2,66},{66,2},{3,67},{67,3},{4,68},{68... | collective-permute-start | bytes 3145736 | tf_op jit(solution)/shard_map/ppermute | solution.py:236
  12.0 7.2 %collective-permute-start = (bf16[4096,128]{1,0:T(8,128)(2,1)S(1)}, bf16[4096,128]{1,0:T(8,128)(2,1)S(1)}, u32[]{:S(2)}, u32[]{:S(2)}) collective-permute-start(bf16[4096,128]{1,0:T(8,128)(2,1)S(1)} %shard_map.41.own_ref), channel_id=1, source_target_pairs={{0,64},{64,0},{1,65},{65,1},{2,66},{66,2},{3,67},{67,3},{4,68},{68... | collective-permute-start | bytes 3145736 | tf_op jit(solution)/shard_map/ppermute | solution.py:236
  15.4 10.9 %all-to-all-start = ((f32[16,24,128]{2,1,0:T(8,128)}), f32[16,24,128]{2,1,0:T(8,128)S(1)}, u32[]{:S(2)}, u32[]{:S(2)}) async-start(f32[16,24,128]{2,1,0:T(8,128)} %bitcast.2), calls=%async_computation | async-start | bytes 393216 | tf_op jit(solution)/shard_map/all_to_all | solution.py:220

commit v4 on v3

v4 whole, which is shorter than its diff:
```python
import functools
import math

import jax
import jax.numpy as jnp
from jax import lax
from jax.experimental import pallas as pl
from jax.experimental.pallas import tpu as pltpu
from jax.sharding import Mesh, PartitionSpec as P

ITERS = 3
NS_STEPS = 6
CHUNK = 1024
ROWS = (((0,), (0,)), ((), ()))
PLAIN = (((1,), (0,)), ((), ()))
COLUMNS = (((1,), (1,)), ((), ()))
bf16 = jnp.bfloat16
f32 = jnp.float32


def dot(a, b, dims=PLAIN):
    return lax.dot_general(a, b, dims, preferred_element_type=f32)


def split(x):
    high = x.astype(bf16)
    return high, (x - high.astype(f32)).astype(bf16)


def wide_dot(a, b, dims=PLAIN):
    (a_high, a_low), (b_high, b_low) = split(a), split(b)
    left = jnp.concatenate([a_high, a_low, a_high], axis=1)
    right = jnp.concatenate([b_high, b_high, b_low], axis=0 if dims is PLAIN else 1)
    return dot(left, right, dims)


def polar_iterate(gram):
    w = gram.shape[0] // 2
    diag = lax.broadcasted_iota(jnp.int32, (w, w), 0) == lax.broadcasted_iota(jnp.int32, (w, w), 1)
    yt = (gram[:w] + gram[w:]) * f32(1.0 / math.sqrt(2.0))
    for outer in range(ITERS):
        scale = 1.0 / (jnp.sum(yt * yt) + 1e-06)
        m = wide_dot(yt, yt, COLUMNS) * scale
        yt = yt * jnp.sqrt(scale)
        ahead = yt if outer == ITERS - 1 else wide_dot(yt, gram)
        square = wide_dot(m, m)
        q = 1.5 * diag.astype(f32) - 0.5 * m
        for inner in range(1, NS_STEPS):
            m = 2.25 * m - 1.5 * square + 0.25 * wide_dot(square, m)
            if inner < NS_STEPS - 1:
                both = wide_dot(jnp.concatenate([m, q], axis=0), m)
                square = both[:w]
                q = 1.5 * q - 0.5 * both[w:]
        u = wide_dot(q, ahead)
        yt = 1.5 * u - 0.5 * wide_dot(m, u)
    return yt


def column_squares(gram, rotation):
    high, rest = split(gram)
    low = (gram - high.astype(f32) - rest.astype(f32)).astype(bf16)
    turned = dot(rotation, high) + (dot(rotation, rest) + dot(rotation, low))
    return jnp.sum((turned * rotation.astype(f32)).T, axis=0, keepdims=True)


def finish_kernel(
    points, core_ref, gram_ref, weights_hbm, bases_ref, near_ref, far_ref,
    out_ref, values_ref, gram_rows_ref, weights_ref, own_ref, other_ref, rows_ref, sem, out_sem,
):
    core = core_ref[0]
    rows, w = own_ref.shape
    half = rows // 2
    here, there = (pl.ds(pl.multiple_of(c * half, half), half) for c in (core, 1 - core))
    loads = [
        pltpu.make_async_copy(bases_ref, own_ref, sem.at[0]),
        pltpu.make_async_copy(near_ref, other_ref.at[here], sem.at[1]),
        pltpu.make_async_copy(far_ref, other_ref.at[there], sem.at[2]),
        pltpu.make_async_copy(weights_hbm, weights_ref, sem.at[3]),
    ]
    for load in loads:
        load.start()
    slices, pairs = gram_ref.shape[:2]
    each = w // slices
    for k in range(slices):
        for p in range(pairs - 1):
            first = k * each + 2 * p if 2 * p < each else w + k * each + 2 * p - each
            gram_rows_ref[first : first + 2] = gram_ref[k, p]
    shared, ab = gram_rows_ref[:w], gram_rows_ref[w:]
    turned = shared.T
    row = lax.broadcasted_iota(jnp.int32, (w, w), 0)
    column = lax.broadcasted_iota(jnp.int32, (w, w), 1)
    aa = jnp.where(row <= column, shared, turned)
    bb = jnp.where(row > column, shared, jnp.where(row < column, turned, gram_ref[0, pairs - 1, :1]))
    gram = jnp.concatenate(
        [jnp.concatenate([aa, ab], axis=1), jnp.concatenate([ab.T, bb], axis=1)], axis=0
    )
    rotation = polar_iterate(gram).astype(bf16)
    squares = column_squares(gram, rotation)
    values = jnp.sqrt(jnp.maximum(squares, 0.0) / points + 1e-06)
    values_ref[...] = values
    inverse = 1.0 / values
    swapped = jnp.concatenate([rotation[:, w:], rotation[:, :w]], axis=1)
    rotation = jnp.where(core == 0, rotation, swapped)
    for load in loads:
        load.wait()
    copies = []
    for j in range(rows // CHUNK):
        part = pl.ds(j * CHUNK, CHUNK)
        own = (own_ref[part].astype(f32) * weights_ref[...]).astype(bf16)
        stacked = jnp.concatenate([own, other_ref[part]], axis=1)
        rows_ref[part] = (dot(stacked, rotation, COLUMNS) * inverse).astype(bf16)
        copies.append(pltpu.make_async_copy(rows_ref.at[part], out_ref.at[part], out_sem.at[j]))
        copies[-1].start()
    for copy in copies:
        copy.wait()


def finish(core, blocks, sing_values, bases, near, far, points):
    rows, w = bases.shape
    vmem = pl.BlockSpec(memory_space=pltpu.VMEM)
    anywhere = pl.BlockSpec(memory_space=pl.ANY)
    return pl.pallas_call(
        functools.partial(finish_kernel, points),
        in_specs=[pl.BlockSpec(memory_space=pltpu.SMEM), vmem]
        + [pl.BlockSpec(memory_space=pltpu.HBM)] * 2
        + [anywhere] * 2,
        out_specs=[anywhere, vmem],
        out_shape=[jax.ShapeDtypeStruct((rows, w), bf16), jax.ShapeDtypeStruct((1, w), f32)],
        scratch_shapes=[
            pltpu.VMEM((2 * w, w), f32),
            pltpu.VMEM(sing_values.shape, f32),
            pltpu.VMEM((rows, w), bf16),
            pltpu.VMEM((rows, w), bf16),
            pltpu.VMEM((rows, w), bf16),
            pltpu.SemaphoreType.DMA((4,)),
            pltpu.SemaphoreType.DMA((rows // CHUNK,)),
        ],
        compiler_params=pltpu.CompilerParams(vmem_limit_bytes=16 << 20),
    )(core, blocks, sing_values, bases, near, far)


def weigh_kernel(
    core_ref, weights_hbm, bases_ref, theirs_ref, mine_ref, weights_ref, rows_ref, sem
):
    rows = bases_ref.shape[0]
    steps = rows // 2 // CHUNK
    weights = pltpu.make_async_copy(weights_hbm, weights_ref, sem.at[2 * steps])
    weights.start()
    copies = []
    for part, block in enumerate((1 - core_ref[0], core_ref[0])):
        for j in range(steps):
            first = pl.multiple_of((block * steps + j) * CHUNK, CHUNK)
            here = rows_ref.at[pl.ds((part * steps + j) * CHUNK, CHUNK)]
            there = bases_ref.at[pl.ds(first, CHUNK)]
            copies.append(pltpu.make_async_copy(there, here, sem.at[part * steps + j]))
            copies[-1].start()
    weights.wait()
    for part, out_ref in enumerate((theirs_ref, mine_ref)):
        for j in range(steps):
            copies[part * steps + j].wait()
            taken = rows_ref[pl.ds((part * steps + j) * CHUNK, CHUNK)]
            out_ref[pl.ds(j * CHUNK, CHUNK)] = (taken.astype(f32) * weights_ref[...]).astype(bf16)


def weigh(core, sing_values, bases):
    rows, w = bases.shape
    vmem = pl.BlockSpec(memory_space=pltpu.VMEM)
    return pl.pallas_call(
        weigh_kernel,
        in_specs=[pl.BlockSpec(memory_space=pltpu.SMEM)] + [pl.BlockSpec(memory_space=pltpu.HBM)] * 2,
        out_specs=[vmem] * 2,
        out_shape=[pltpu.VMEM((rows // 2, w), bf16)] * 2,
        scratch_shapes=[
            pltpu.VMEM(sing_values.shape, f32),
            pltpu.VMEM((rows, w), bf16),
            pltpu.SemaphoreType.DMA((rows // CHUNK + 1,)),
        ],
        compiler_params=pltpu.CompilerParams(vmem_limit_bytes=8 << 20),
    )(core, sing_values, bases)


def gram_kernel(own_ref, other_ref, out_ref):
    stacked = jnp.concatenate([own_ref[...], other_ref[...]], axis=1)
    out_ref[...] = dot(stacked, stacked, ROWS)


def half_gram(own, other):
    w = own.shape[1]
    vmem = pl.BlockSpec(memory_space=pltpu.VMEM)
    return pl.pallas_call(
        gram_kernel,
        in_specs=[vmem, vmem],
        out_specs=vmem,
        out_shape=jax.ShapeDtypeStruct((2 * w, 2 * w), f32),
        compiler_params=pltpu.CompilerParams(vmem_limit_bytes=8 << 20),
    )(own, other)


def pack_kernel(core_ref, after_ref, gram_ref, out_ref):
    w = gram_ref.shape[0] // 2
    even = core_ref[0] == 0
    own, other = gram_ref[:w, :w], gram_ref[w:, w:]
    across = jnp.where(even, gram_ref[:w, w:], gram_ref[w:, :w])
    aa, bb = jnp.where(even, own, other), jnp.where(even, other, own)
    row = lax.broadcasted_iota(jnp.int32, (w, w), 0)
    column = lax.broadcasted_iota(jnp.int32, (w, w), 1)
    shared = jnp.where(row <= column, aa, bb)
    diag = jnp.sum(jnp.where(row == column, bb, 0.0), axis=0, keepdims=True)
    slices, pairs = out_ref.shape[:2]
    each = w // slices
    for k in range(slices):
        for p in range(each // 2):
            first = k * each + 2 * p
            out_ref[k, p] = shared[first : first + 2]
            out_ref[k, each // 2 + p] = across[first : first + 2]
        out_ref[k, pairs - 1] = jnp.broadcast_to(diag, (2, w))


def pack(core, gram, slices, after):
    w = gram.shape[0] // 2
    vmem = pl.BlockSpec(memory_space=pltpu.VMEM)
    return pl.pallas_call(
        pack_kernel,
        in_specs=[
            pl.BlockSpec(memory_space=pltpu.SMEM),
            pl.BlockSpec(memory_space=pl.ANY),
            vmem,
        ],
        out_specs=vmem,
        out_shape=jax.ShapeDtypeStruct((slices, w // slices + 1, 2, w), f32),
        compiler_params=pltpu.CompilerParams(vmem_limit_bytes=4 << 20),
    )(core, after, gram)


def sum_over_chips(part):
    near, far = ("core", "z_lo", "x"), "z_hi"
    n, m = part.shape[0], lax.axis_size(far)
    turned = [[(i + m // 2) % m for i in range(m)]]
    part = lax.all_to_all(part, near, 0, 0)
    part = jnp.broadcast_to(jnp.sum(part, axis=0)[None], (m, *part.shape[1:]))
    part = lax.all_to_all(part, far, 0, 0, axis_index_groups=turned)
    part = jnp.broadcast_to(jnp.sum(part, axis=0)[None], (n, *part.shape[1:]))
    return lax.all_to_all(part, near, 0, 0)


def local(bases, sing_values):
    rows = bases.shape[1]
    points = rows * math.prod(lax.axis_size(axis) for axis in ("z_hi", "z_lo", "x"))
    core = lax.axis_index("core").astype(jnp.int32)

    def partners(value):
        return lax.ppermute(value, "core", [(0, 1), (1, 0)])

    bases = pltpu.with_memory_space_constraint(bases[0], pltpu.HBM)
    sing_values = pltpu.with_memory_space_constraint(sing_values, pltpu.HBM)
    theirs, mine = weigh(core[None], sing_values, bases)
    other_a = partners(theirs)
    other_b = partners(mine)
    slices = math.prod(lax.axis_size(axis) for axis in ("core", "z_lo", "x"))
    blocks = sum_over_chips(pack(core[None], half_gram(mine, other_a), slices, other_b))
    merged, values = finish(
        core[None], blocks, sing_values, bases, other_a, other_b, points
    )
    return (merged[None], values)


def solution(mesh):
    fine = Mesh(mesh.devices.reshape(-1, 2, 8, 2, 4), ("y", "core", "z_hi", "z_lo", "x"))
    specs = (P(("y", "core"), ("z_hi", "z_lo", "x"), None), P(("y", "core"), None))
    return jax.shard_map(local, mesh=fine, in_specs=specs, out_specs=specs, check_vma=False)
```

time: 65.8 us -> 63.2 us (0.960)
  blocking collectives: 29.2 us -> 37.6 us
  waiting for transfers between devices: 7.05 us -> 1.86 us
  starting transfers between devices: 14.6 us -> 10.7 us
  Pallas kernels: 13.9 us -> 11.8 us
    all_to_all x1 -> x2, blocking collectives: 11.2 us -> 19.8 us  [the longest x1 10.7 us: sum_over_chips(): return lax.all_to_all(part, near, 0, 0)]
    all_to_all x1 -> x0, waiting for transfers between devices: 7.05 us -> none  [sum_over_chips(): part = lax.all_to_all(part.reshape(n, rows // n, w), near, 0, 0)]
    all_to_all x1 -> x0, starting transfers between devices: 3.85 us -> none  [sum_over_chips(): part = lax.all_to_all(part.reshape(n, rows // n, w), near, 0, 0)]
    ppermute x2, waiting for transfers between devices: 0.01 us -> 1.86 us  [partners(): return lax.ppermute(value, 'core', [(0, 1), (1, 0)])]
    pallas_call x4 -> x3, Pallas kernels: 4.06 us -> 2.43 us  [the longest x1 1.64 us: weigh(): pl.pallas_call(weigh_kernel, in_specs=[pl.BlockSpec(memory_space=pltpu.SM...]
  transfers between devices with their start and end apart: 3 -> 2, of which waited for: 1 -> 2; matrix products, arithmetic and copies ran while one was open for 0% -> 0% of each run, Pallas kernels for 4% -> 1%
where the time goes in v4:
time: 63.2 us; the launch traced here: 62.9 us
  blocking collectives  37.6 us (59%)
  Pallas kernels  11.8 us (19%)
  starting transfers between devices  10.7 us (17%)
  waiting for transfers between devices  1.86 us (3%)
  between operations  0.68 us (1%)
    all_to_all x1, blocking collectives, sum_over_chips(): part = lax.all_to_all(part, far, 0, 0, axis_index_groups=turned)  17.9 us
    ppermute x2, starting transfers between devices, partners(): return lax.ppermute(value, 'core', [(0, 1), (1, 0)])  10.7 us
    all_to_all x1, blocking collectives, sum_over_chips(): return lax.all_to_all(part, near, 0, 0)  10.7 us
    pallas_call x1, Pallas kernels, finish(): pl.pallas_call(functools.partial(finish_kernel, points), in_specs=[pl.Blo...  9.39 us
    all_to_all x1, blocking collectives, sum_over_chips(): part = lax.all_to_all(part, near, 0, 0)  9.11 us
    ppermute x2, waiting for transfers between devices, partners(): return lax.ppermute(value, 'core', [(0, 1), (1, 0)])  1.86 us
    pallas_call x1, Pallas kernels, weigh(): pl.pallas_call(weigh_kernel, in_specs=[pl.BlockSpec(memory_space=pltpu.SM...  1.64 us
  transfers between devices with their start and end apart: 2, of which 2 were waited for; matrix products, arithmetic and copies ran while one was open for 0% of the time, Pallas kernels for 1%

profile of v4, /device:TPU:1, one launch (start us, length us, event | category | flops | bytes accessed | tf_op | source)
XLA Modules:
  0.0 62.9 jit_solution(208422123079182934)
XLA Ops:
  0.6 1.6 %shard_map.41 = (bf16[4096,128]{1,0:T(8,128)(2,1)S(1)}, bf16[4096,128]{1,0:T(8,128)(2,1)S(1)}) custom-call(s32[1]{0:T(128)} %bitcast.core_ref, f32[1,128]{1,0:T(1,128)} %weights_hbm.3, bf16[8192,128]{1,0:T(8,128)(2,1)} %bitcast.3), custom_call_target="tpu_custom_call" | custom-call | tf_op jit(solution)/shard_map/pallas_call | solution.py:168
  2.3 8.8 %collective-permute-start.1 = (bf16[4096,128]{1,0:T(8,128)(2,1)S(1)}, bf16[4096,128]{1,0:T(8,128)(2,1)S(1)}, u32[]{:S(2)}, u32[]{:S(2)}) collective-permute-start(bf16[4096,128]{1,0:T(8,128)(2,1)S(1)} %get-tuple-element.7), channel_id=1, source_target_pairs={{0,64},{64,0},{1,65},{65,1},{2,66},{66,2},{3,67},{67,3},{4,68},{68... | collective-permute-start | bytes 3145736 | tf_op jit(solution)/shard_map/ppermute | solution.py:252
  11.1 1.9 %collective-permute-start = (bf16[4096,128]{1,0:T(8,128)(2,1)S(1)}, bf16[4096,128]{1,0:T(8,128)(2,1)S(1)}, u32[]{:S(2)}, u32[]{:S(2)}) collective-permute-start(bf16[4096,128]{1,0:T(8,128)(2,1)S(1)} %get-tuple-element.6.own_ref), channel_id=1, source_target_pairs={{0,64},{64,0},{1,65},{65,1},{2,66},{66,2},{3,67},{67,3},{4,68},{68... | collective-permute-start | bytes 3145736 | tf_op jit(solution)/shard_map/ppermute | solution.py:252
  13.0 0.3 collective-permute-done.1.other_ref.near_ref
  13.3 0.8 %shard_map.42.gram_ref = f32[256,256]{1,0:T(8,128)S(1)} custom-call(bf16[4096,128]{1,0:T(8,128)(2,1)S(1)} %get-tuple-element.6.own_ref, bf16[4096,128]{1,0:T(8,128)(2,1)S(1)} %collective-permute-done.1.other_ref.near_ref), custom_call_target="tpu_custom_call" | custom-call | tf_op jit(solution)/shard_map/pallas_call | solution.py:190
  14.1 1.5 %collective-permute-done.after_ref.far_ref = bf16[4096,128]{1,0:T(8,128)(2,1)S(1)} collective-permute-done((bf16[4096,128]{1,0:T(8,128)(2,1)S(1)}, bf16[4096,128]{1,0:T(8,128)(2,1)S(1)}, u32[]{:S(2)}, u32[]{:S(2)}) %collective-permute-start) | collective-permute-done | bytes 1048608 | tf_op jit(solution)/shard_map/ppermute | solution.py:252
  15.7 9.1 %all_to_all.15 = f32[16,9,2,128]{3,2,1,0:T(2,128)S(1)} all-to-all(f32[16,9,2,128]{3,2,1,0:T(2,128)S(1)} %shard_map.43), channel_id=1, replica_groups=mesh['y'=4,'core'=2,'z_hi'=8,'z_lo'=2,'x'=4] {'core','z_lo','x'}, dimensions={0} | all-to-all | bytes 294912 | tf_op jit(solution)/shard_map/all_to_all | solution.py:239
  24.8 0.1 reduce_sum.18
  24.9 17.9 %all_to_all.16 = f32[8,9,2,128]{3,2,1,0:T(2,128)S(1)} all-to-all(f32[8,9,2,128]{3,2,1,0:T(2,128)S(1)} %broadcast_in_dim.9), channel_id=1, replica_groups={{32,40,48,56,0,8,16,24},{33,41,49,57,1,9,17,25},{34,42,50,58,2,10,18,26..., dimensions={0} | all-to-all | bytes 147456 | tf_op jit(solution)/shard_map/all_to_all | solution.py:241
  42.8 10.7 %all_to_all.17.gram_ref = f32[16,9,2,128]{3,2,1,0:T(2,128)S(1)} all-to-all(f32[16,9,2,128]{3,2,1,0:T(2,128)S(1)} %broadcast_in_dim.10), channel_id=1, replica_groups=mesh['y'=4,'core'=2,'z_hi'=8,'z_lo'=2,'x'=4] {'core','z_lo','x'}, dimensions={0} | all-to-all | bytes 294912 | tf_op jit(solution)/shard_map/all_to_all | solution.py:243
  53.5 9.4 %shard_map.44 = (bf16[8192,128]{1,0:T(8,128)(2,1)}, f32[1,128]{1,0:T(1,128)}) custom-call(s32[1]{0:T(128)} %bitcast.core_ref, f32[16,9,2,128]{3,2,1,0:T(2,128)S(1)} %all_to_all.17.gram_ref, f32[1,128]{1,0:T(1,128)} %weights_hbm.3, bf16[8192,128]{1,0:T(8,128)(2,1)} %bitcast.4, bf16[4096,128]{1,0:T(8,128)(2,1)S(1)} %collective-permute-done.1.other_ref.near_ref, ...), custom_call_target="tpu_custom_call" | custom-call | tf_op jit(solution)/shard_map/pallas_call | solution.py:122
  (4 shorter events, 0.1 us)
Async XLA Ops:
  2.3 11.1 %collective-permute-start.1 = (bf16[4096,128]{1,0:T(8,128)(2,1)S(1)}, bf16[4096,128]{1,0:T(8,128)(2,1)S(1)}, u32[]{:S(2)}, u32[]{:S(2)}) collective-permute-start(bf16[4096,128]{1,0:T(8,128)(2,1)S(1)} %get-tuple-element.7), channel_id=1, source_target_pairs={{0,64},{64,0},{1,65},{65,1},{2,66},{66,2},{3,67},{67,3},{4,68},{68... | collective-permute-start | bytes 3145736 | tf_op jit(solution)/shard_map/ppermute | solution.py:252
  11.1 4.6 %collective-permute-start = (bf16[4096,128]{1,0:T(8,128)(2,1)S(1)}, bf16[4096,128]{1,0:T(8,128)(2,1)S(1)}, u32[]{:S(2)}, u32[]{:S(2)}) collective-permute-start(bf16[4096,128]{1,0:T(8,128)(2,1)S(1)} %get-tuple-element.6.own_ref), channel_id=1, source_target_pairs={{0,64},{64,0},{1,65},{65,1},{2,66},{66,2},{3,67},{67,3},{4,68},{68... | collective-permute-start | bytes 3145736 | tf_op jit(solution)/shard_map/ppermute | solution.py:252

commit v5 on v4

v5 whole, which is shorter than its diff:
```python
import functools
import math

import jax
import jax.numpy as jnp
from jax import lax
from jax.experimental import pallas as pl
from jax.experimental.pallas import tpu as pltpu
from jax.sharding import Mesh, PartitionSpec as P

ITERS = 3
NS_STEPS = 6
CHUNK = 1024
ROWS = (((0,), (0,)), ((), ()))
PLAIN = (((1,), (0,)), ((), ()))
COLUMNS = (((1,), (1,)), ((), ()))
bf16 = jnp.bfloat16
f32 = jnp.float32


def dot(a, b, dims=PLAIN):
    return lax.dot_general(a, b, dims, preferred_element_type=f32)


def split(x):
    high = x.astype(bf16)
    return high, (x - high.astype(f32)).astype(bf16)


def wide_dot(a, b, dims=PLAIN):
    (a_high, a_low), (b_high, b_low) = split(a), split(b)
    left = jnp.concatenate([a_high, a_low, a_high], axis=1)
    right = jnp.concatenate([b_high, b_high, b_low], axis=0 if dims is PLAIN else 1)
    return dot(left, right, dims)


def polar_iterate(gram):
    w = gram.shape[0] // 2
    diag = lax.broadcasted_iota(jnp.int32, (w, w), 0) == lax.broadcasted_iota(jnp.int32, (w, w), 1)
    yt = (gram[:w] + gram[w:]) * f32(1.0 / math.sqrt(2.0))
    for outer in range(ITERS):
        scale = 1.0 / (jnp.sum(yt * yt) + 1e-06)
        m = wide_dot(yt, yt, COLUMNS) * scale
        yt = yt * jnp.sqrt(scale)
        last = outer == ITERS - 1
        ahead = yt.T if last else wide_dot(yt, gram)
        square = wide_dot(m, m)
        q = 1.5 * diag.astype(f32) - 0.5 * m
        for inner in range(1, NS_STEPS):
            m = 2.25 * m - 1.5 * square + 0.25 * wide_dot(square, m)
            if inner < NS_STEPS - 1:
                both = wide_dot(jnp.concatenate([m, q], axis=0), m)
                square = both[:w]
                q = 1.5 * q - 0.5 * both[w:]
        u = wide_dot(ahead, q) if last else wide_dot(q, ahead)
        yt = 1.5 * u - 0.5 * (wide_dot(u, m) if last else wide_dot(m, u))
    return yt


def column_squares(gram, rotation):
    high, rest = split(gram)
    low = (gram - high.astype(f32) - rest.astype(f32)).astype(bf16)
    turned = dot(high, rotation) + (dot(rest, rotation) + dot(low, rotation))
    return jnp.sum(turned * rotation.astype(f32), axis=0, keepdims=True)


def weighted(rows, weights_ref):
    return (rows.astype(f32) * weights_ref[...]).astype(bf16)


def finish_kernel(
    points, core_ref, gram_ref, other_weights_ref, weights_hbm, bases_ref, others_ref,
    out_ref, values_ref, gram_rows_ref, weights_ref, own_ref, other_ref, rows_ref, sem, out_sem,
):
    core = core_ref[0]
    rows, w = own_ref.shape
    loads = [
        pltpu.make_async_copy(bases_ref, own_ref, sem.at[0]),
        pltpu.make_async_copy(others_ref, other_ref, sem.at[1]),
        pltpu.make_async_copy(weights_hbm, weights_ref, sem.at[2]),
    ]
    for load in loads:
        load.start()
    slices, pairs = gram_ref.shape[:2]
    each = w // slices
    for k in range(slices):
        for p in range(pairs - 1):
            first = k * each + 2 * p if 2 * p < each else w + k * each + 2 * p - each
            gram_rows_ref[first : first + 2] = gram_ref[k, p]
    shared, ab = gram_rows_ref[:w], gram_rows_ref[w:]
    turned = shared.T
    row = lax.broadcasted_iota(jnp.int32, (w, w), 0)
    column = lax.broadcasted_iota(jnp.int32, (w, w), 1)
    aa = jnp.where(row <= column, shared, turned)
    bb = jnp.where(row > column, shared, jnp.where(row < column, turned, gram_ref[0, pairs - 1, :1]))
    gram = jnp.concatenate(
        [jnp.concatenate([aa, ab], axis=1), jnp.concatenate([ab.T, bb], axis=1)], axis=0
    )
    rotation = polar_iterate(gram).astype(bf16)
    squares = column_squares(gram, rotation)
    values = jnp.sqrt(jnp.maximum(squares, 0.0) / points + 1e-06)
    values_ref[...] = values
    inverse = 1.0 / values
    swapped = jnp.concatenate([rotation[w:], rotation[:w]], axis=0)
    rotation = jnp.where(core == 0, rotation, swapped)
    for load in loads:
        load.wait()
    copies = []
    for j in range(rows // CHUNK):
        part = pl.ds(j * CHUNK, CHUNK)
        own = weighted(own_ref[part], weights_ref)
        stacked = jnp.concatenate([own, weighted(other_ref[part], other_weights_ref)], axis=1)
        rows_ref[part] = (dot(stacked, rotation) * inverse).astype(bf16)
        copies.append(pltpu.make_async_copy(rows_ref.at[part], out_ref.at[part], out_sem.at[j]))
        copies[-1].start()
    for copy in copies:
        copy.wait()


def finish(core, blocks, other_values, sing_values, bases, others, points):
    rows, w = bases.shape
    smem, vmem, hbm, anywhere = (
        pl.BlockSpec(memory_space=space) for space in (pltpu.SMEM, pltpu.VMEM, pltpu.HBM, pl.ANY)
    )
    return pl.pallas_call(
        functools.partial(finish_kernel, points),
        in_specs=[smem, vmem, vmem, hbm, hbm, anywhere],
        out_specs=[anywhere, vmem],
        out_shape=[jax.ShapeDtypeStruct((rows, w), bf16), jax.ShapeDtypeStruct((1, w), f32)],
        scratch_shapes=[
            pltpu.VMEM((2 * w, w), f32),
            pltpu.VMEM(sing_values.shape, f32),
            pltpu.VMEM((rows, w), bf16),
            pltpu.VMEM((rows, w), bf16),
            pltpu.VMEM((rows, w), bf16),
            pltpu.SemaphoreType.DMA((3,)),
            pltpu.SemaphoreType.DMA((rows // CHUNK,)),
        ],
        compiler_params=pltpu.CompilerParams(vmem_limit_bytes=16 << 20),
    )(core, blocks, other_values, sing_values, bases, others)


def weigh_kernel(core_ref, weights_hbm, bases_ref, out_ref, weights_ref, rows_ref, sem):
    half = out_ref.shape[0]
    steps = half // CHUNK
    weights = pltpu.make_async_copy(weights_hbm, weights_ref, sem.at[steps])
    weights.start()
    copies = []
    for j in range(steps):
        first = pl.multiple_of((core_ref[0] * steps + j) * CHUNK, CHUNK)
        here = rows_ref.at[pl.ds(j * CHUNK, CHUNK)]
        copies.append(pltpu.make_async_copy(bases_ref.at[pl.ds(first, CHUNK)], here, sem.at[j]))
        copies[-1].start()
    weights.wait()
    for j, copy in enumerate(copies):
        copy.wait()
        part = pl.ds(j * CHUNK, CHUNK)
        out_ref[part] = weighted(rows_ref[part], weights_ref)


def weigh(core, sing_values, bases):
    rows, w = bases.shape
    vmem, hbm = (pl.BlockSpec(memory_space=space) for space in (pltpu.VMEM, pltpu.HBM))
    return pl.pallas_call(
        weigh_kernel,
        in_specs=[pl.BlockSpec(memory_space=pltpu.SMEM), hbm, hbm],
        out_specs=vmem,
        out_shape=pltpu.VMEM((rows // 2, w), bf16),
        scratch_shapes=[
            pltpu.VMEM(sing_values.shape, f32),
            pltpu.VMEM((rows // 2, w), bf16),
            pltpu.SemaphoreType.DMA((rows // 2 // CHUNK + 1,)),
        ],
        compiler_params=pltpu.CompilerParams(vmem_limit_bytes=8 << 20),
    )(core, sing_values, bases)


def gram_kernel(core_ref, own_ref, others_ref, other_weights_ref, out_ref):
    half, w = own_ref.shape
    first = pl.multiple_of(core_ref[0] * half, half)
    other = weighted(others_ref[pl.ds(first, half)], other_weights_ref)
    stacked = jnp.concatenate([own_ref[...], other], axis=1)
    gram = dot(stacked, stacked, ROWS)
    even = core_ref[0] == 0
    own, other = gram[:w, :w], gram[w:, w:]
    across = jnp.where(even, gram[:w, w:], gram[w:, :w])
    aa, bb = jnp.where(even, own, other), jnp.where(even, other, own)
    row = lax.broadcasted_iota(jnp.int32, (w, w), 0)
    column = lax.broadcasted_iota(jnp.int32, (w, w), 1)
    shared = jnp.where(row <= column, aa, bb)
    diag = jnp.sum(jnp.where(row == column, bb, 0.0), axis=0, keepdims=True)
    slices, pairs = out_ref.shape[:2]
    each = w // slices
    for k in range(slices):
        for p in range(each // 2):
            first = k * each + 2 * p
            out_ref[k, p] = shared[first : first + 2]
            out_ref[k, each // 2 + p] = across[first : first + 2]
        out_ref[k, pairs - 1] = jnp.broadcast_to(diag, (2, w))


def half_gram(core, own, others, other_values, slices):
    w = own.shape[1]
    vmem = pl.BlockSpec(memory_space=pltpu.VMEM)
    return pl.pallas_call(
        gram_kernel,
        in_specs=[pl.BlockSpec(memory_space=pltpu.SMEM)] + [vmem] * 3,
        out_specs=vmem,
        out_shape=jax.ShapeDtypeStruct((slices, w // slices + 1, 2, w), f32),
        compiler_params=pltpu.CompilerParams(vmem_limit_bytes=12 << 20),
    )(core, own, others, other_values)


def sum_over_chips(part):
    near, far = ("core", "z_lo", "x"), "z_hi"
    n, m = part.shape[0], lax.axis_size(far)
    turned = [[(i + m // 2) % m for i in range(m)]]
    part = lax.all_to_all(part, near, 0, 0)
    part = jnp.broadcast_to(jnp.sum(part, axis=0)[None], (m, *part.shape[1:]))
    part = lax.all_to_all(part, far, 0, 0, axis_index_groups=turned)
    part = jnp.broadcast_to(jnp.sum(part, axis=0)[None], (n, *part.shape[1:]))
    return lax.all_to_all(part, near, 0, 0)


def local(bases, sing_values):
    rows = bases.shape[1]
    points = rows * math.prod(lax.axis_size(axis) for axis in ("z_hi", "z_lo", "x"))
    core = lax.axis_index("core").astype(jnp.int32)

    def partners(value):
        return lax.ppermute(value, "core", [(0, 1), (1, 0)])

    others, other_values = partners(bases[0]), partners(sing_values)
    bases = pltpu.with_memory_space_constraint(bases[0], pltpu.HBM)
    sing_values = pltpu.with_memory_space_constraint(sing_values, pltpu.HBM)
    mine = weigh(core[None], sing_values, bases)
    slices = math.prod(lax.axis_size(axis) for axis in ("core", "z_lo", "x"))
    blocks = sum_over_chips(half_gram(core[None], mine, others, other_values, slices))
    merged, values = finish(core[None], blocks, other_values, sing_values, bases, others, points)
    return (merged[None], values)


def solution(mesh):
    fine = Mesh(mesh.devices.reshape(-1, 2, 8, 2, 4), ("y", "core", "z_hi", "z_lo", "x"))
    specs = (P(("y", "core"), ("z_hi", "z_lo", "x"), None), P(("y", "core"), None))
    return jax.shard_map(local, mesh=fine, in_specs=specs, out_specs=specs, check_vma=False)
```

time: 63.2 us -> 61.9 us (0.979)
  waiting for transfers between devices: 1.86 us -> 0.74 us
    ppermute x2, waiting for transfers between devices: 1.86 us -> 0.74 us  [partners(): return lax.ppermute(value, 'core', [(0, 1), (1, 0)])]
    pallas_call x3 -> x2, Pallas kernels: 10.2 us -> 10.2 us  [the longest x1 9.43 us: finish(): pl.pallas_call(functools.partial(finish_kernel, points), in_specs=[smem,...]
  transfers between devices with their start and end apart: 2 -> 2, of which waited for: 2 -> 1; matrix products, arithmetic and copies ran while one was open for 0% -> 0% of each run, Pallas kernels for 1% -> 2%
where the time goes in v5:
time: 61.9 us; the launch traced here: 61.6 us
  blocking collectives  37.9 us (61%)
  Pallas kernels  11.5 us (19%)
  starting transfers between devices  10.7 us (17%)
  waiting for transfers between devices  0.74 us (1%)
  between operations  0.67 us (1%)
    all_to_all x1, blocking collectives, sum_over_chips(): part = lax.all_to_all(part, far, 0, 0, axis_index_groups=turned)  17.8 us
    ppermute x2, starting transfers between devices, partners(): return lax.ppermute(value, 'core', [(0, 1), (1, 0)])  10.7 us
    all_to_all x1, blocking collectives, sum_over_chips(): return lax.all_to_all(part, near, 0, 0)  10.7 us
    pallas_call x1, Pallas kernels, finish(): pl.pallas_call(functools.partial(finish_kernel, points), in_specs=[smem,...  9.43 us
    all_to_all x1, blocking collectives, sum_over_chips(): part = lax.all_to_all(part, near, 0, 0)  9.36 us
    pallas_call x1, Pallas kernels, weigh(): pl.pallas_call(weigh_kernel, in_specs=[pl.BlockSpec(memory_space=pltpu.SM...  1.29 us
  transfers between devices with their start and end apart: 2, of which 1 were waited for; matrix products, arithmetic and copies ran while one was open for 0% of the time, Pallas kernels for 2%

profile of v5, /device:TPU:1, one launch (start us, length us, event | category | flops | bytes accessed | tf_op | source)
XLA Modules:
  0.0 61.6 jit_solution(12368284640488077293)
XLA Ops:
  0.6 8.8 %collective-permute-start = (bf16[8192,128]{1,0:T(8,128)(2,1)}, bf16[8192,128]{1,0:T(8,128)(2,1)S(1)}, u32[]{:S(2)}, u32[]{:S(2)}) collective-permute-start(bf16[8192,128]{1,0:T(8,128)(2,1)} %bitcast.3), channel_id=1, source_target_pairs={{0,64},{64,0},{1,65},{65,1},{2,66},{66,2},{3,67},{67,3},{4,68},{68... | collective-permute-start | bytes 6291464 | tf_op jit(solution)/shard_map/ppermute | solution.py:231
  9.4 1.9 %collective-permute-start.1 = (f32[1,128]{1,0:T(1,128)}, f32[1,128]{1,0:T(1,128)S(1)}, u32[]{:S(2)}, u32[]{:S(2)}) collective-permute-start(f32[1,128]{1,0:T(1,128)} %weights_hbm.3), channel_id=1, source_target_pairs={{0,64},{64,0},{1,65},{65,1},{2,66},{66,2},{3,67},{67,3},{4,68},{68... | collective-permute-start | bytes 1544 | tf_op jit(solution)/shard_map/ppermute | solution.py:231
  11.4 1.3 %shard_map.41.own_ref = bf16[4096,128]{1,0:T(8,128)(2,1)S(1)} custom-call(s32[1]{0:T(128)} %bitcast.core_ref, f32[1,128]{1,0:T(1,128)} %weights_hbm.3, bf16[8192,128]{1,0:T(8,128)(2,1)} %bitcast.4), custom_call_target="tpu_custom_call" | custom-call | tf_op jit(solution)/shard_map/pallas_call | solution.py:164
  12.7 0.7 %collective-permute-done.1.other_weights_ref = f32[1,128]{1,0:T(1,128)S(1)} collective-permute-done((f32[1,128]{1,0:T(1,128)}, f32[1,128]{1,0:T(1,128)S(1)}, u32[]{:S(2)}, u32[]{:S(2)}) %collective-permute-start.1) | collective-permute-done | bytes 544 | tf_op jit(solution)/shard_map/ppermute | solution.py:231
  13.4 0.0 collective-permute-done.others_ref
  13.4 0.8 %shard_map.42 = f32[16,9,2,128]{3,2,1,0:T(2,128)S(1)} custom-call(s32[1]{0:T(128)} %bitcast.core_ref, bf16[4096,128]{1,0:T(8,128)(2,1)S(1)} %shard_map.41.own_ref, bf16[8192,128]{1,0:T(8,128)(2,1)S(1)} %collective-permute-done.others_ref, f32[1,128]{1,0:T(1,128)S(1)} %collective-permute-done.1.other_weights_ref), custom_call_target="tpu_custom_call" | custom-call | tf_op jit(solution)/shard_map/pallas_call | solution.py:205
  14.2 9.4 %all_to_all.15 = f32[16,9,2,128]{3,2,1,0:T(2,128)S(1)} all-to-all(f32[16,9,2,128]{3,2,1,0:T(2,128)S(1)} %shard_map.42), channel_id=1, replica_groups=mesh['y'=4,'core'=2,'z_hi'=8,'z_lo'=2,'x'=4] {'core','z_lo','x'}, dimensions={0} | all-to-all | bytes 294912 | tf_op jit(solution)/shard_map/all_to_all | solution.py:218
  23.5 0.1 reduce_sum.18
  23.6 17.8 %all_to_all.16 = f32[8,9,2,128]{3,2,1,0:T(2,128)S(1)} all-to-all(f32[8,9,2,128]{3,2,1,0:T(2,128)S(1)} %broadcast_in_dim.9), channel_id=1, replica_groups={{32,40,48,56,0,8,16,24},{33,41,49,57,1,9,17,25},{34,42,50,58,2,10,18,26..., dimensions={0} | all-to-all | bytes 147456 | tf_op jit(solution)/shard_map/all_to_all | solution.py:220
  41.5 10.7 %all_to_all.17.gram_ref = f32[16,9,2,128]{3,2,1,0:T(2,128)S(1)} all-to-all(f32[16,9,2,128]{3,2,1,0:T(2,128)S(1)} %broadcast_in_dim.10), channel_id=1, replica_groups=mesh['y'=4,'core'=2,'z_hi'=8,'z_lo'=2,'x'=4] {'core','z_lo','x'}, dimensions={0} | all-to-all | bytes 294912 | tf_op jit(solution)/shard_map/all_to_all | solution.py:222
  52.2 9.4 %shard_map.43 = (bf16[8192,128]{1,0:T(8,128)(2,1)}, f32[1,128]{1,0:T(1,128)}) custom-call(s32[1]{0:T(128)} %bitcast.core_ref, f32[16,9,2,128]{3,2,1,0:T(2,128)S(1)} %all_to_all.17.gram_ref, f32[1,128]{1,0:T(1,128)S(1)} %collective-permute-done.1.other_weights_ref, f32[1,128]{1,0:T(1,128)} %weights_hbm.3, bf16[8192,128]{1,0:T(8,128)(2,1)} %bitcast.5, ...), custom_call_target="tpu_custom_call" | custom-call | tf_op jit(solution)/shard_map/pallas_call | solution.py:125
  (3 shorter events, 0.1 us)
Async XLA Ops:
  0.6 12.8 %collective-permute-start = (bf16[8192,128]{1,0:T(8,128)(2,1)}, bf16[8192,128]{1,0:T(8,128)(2,1)S(1)}, u32[]{:S(2)}, u32[]{:S(2)}) collective-permute-start(bf16[8192,128]{1,0:T(8,128)(2,1)} %bitcast.3), channel_id=1, source_target_pairs={{0,64},{64,0},{1,65},{65,1},{2,66},{66,2},{3,67},{67,3},{4,68},{68... | collective-permute-start | bytes 6291464 | tf_op jit(solution)/shard_map/ppermute | solution.py:231
  9.4 4.0 %collective-permute-start.1 = (f32[1,128]{1,0:T(1,128)}, f32[1,128]{1,0:T(1,128)S(1)}, u32[]{:S(2)}, u32[]{:S(2)}) collective-permute-start(f32[1,128]{1,0:T(1,128)} %weights_hbm.3), channel_id=1, source_target_pairs={{0,64},{64,0},{1,65},{65,1},{2,66},{66,2},{3,67},{67,3},{4,68},{68... | collective-permute-start | bytes 1544 | tf_op jit(solution)/shard_map/ppermute | solution.py:231

commit v6 on v5

--- a/solution.py
+++ b/solution.py
@@ -11,6 +11,7 @@
 ITERS = 3
 NS_STEPS = 6
 CHUNK = 1024
+FIRST = 10
 ROWS = (((0,), (0,)), ((), ()))
 PLAIN = (((1,), (0,)), ((), ()))
 COLUMNS = (((1,), (1,)), ((), ()))
@@ -97,14 +98,14 @@
         [jnp.concatenate([aa, ab], axis=1), jnp.concatenate([ab.T, bb], axis=1)], axis=0
     )
     rotation = polar_iterate(gram).astype(bf16)
+    for load in loads:
+        load.wait()
     squares = column_squares(gram, rotation)
     values = jnp.sqrt(jnp.maximum(squares, 0.0) / points + 1e-06)
     values_ref[...] = values
     inverse = 1.0 / values
     swapped = jnp.concatenate([rotation[w:], rotation[:w]], axis=0)
     rotation = jnp.where(core == 0, rotation, swapped)
-    for load in loads:
-        load.wait()
     copies = []
     for j in range(rows // CHUNK):
         part = pl.ds(j * CHUNK, CHUNK)
@@ -194,8 +195,8 @@
     for k in range(slices):
         for p in range(each // 2):
             first = k * each + 2 * p
-            out_ref[k, p] = shared[first : first + 2]
-            out_ref[k, each // 2 + p] = across[first : first + 2]
+            out_ref[(k - FIRST) % slices, p] = shared[first : first + 2]
+            out_ref[(k - FIRST) % slices, each // 2 + p] = across[first : first + 2]
         out_ref[k, pairs - 1] = jnp.broadcast_to(diag, (2, w))
 
 
@@ -215,7 +216,8 @@
     near, far = ("core", "z_lo", "x"), "z_hi"
     n, m = part.shape[0], lax.axis_size(far)
     turned = [[(i + m // 2) % m for i in range(m)]]
-    part = lax.all_to_all(part, near, 0, 0)
+    near_turned = [[(i + FIRST) % n for i in range(n)]]
+    part = lax.all_to_all(part, near, 0, 0, axis_index_groups=near_turned)
     part = jnp.broadcast_to(jnp.sum(part, axis=0)[None], (m, *part.shape[1:]))
     part = lax.all_to_all(part, far, 0, 0, axis_index_groups=turned)
     part = jnp.broadcast_to(jnp.sum(part, axis=0)[None], (n, *part.shape[1:]))

time: 61.9 us -> 61.2 us (0.989)
    all_to_all x1, blocking collectives: 10.7 us -> 12 us  [sum_over_chips(): return lax.all_to_all(part, near, 0, 0)]
    all_to_all x1, blocking collectives: 9.36 us -> 8.23 us  [sum_over_chips(): part = lax.all_to_all(part, near, 0, 0, axis_index_groups=near_turned)]
    all_to_all x1, blocking collectives: 17.8 us -> 17.2 us  [sum_over_chips(): part = lax.all_to_all(part, far, 0, 0, axis_index_groups=turned)]
where the time goes in v6:
time: 61.2 us; the launch traced here: 60.9 us
  blocking collectives  37.4 us (61%)
  Pallas kernels  11.2 us (18%)
  starting transfers between devices  10.7 us (17%)
  waiting for transfers between devices  0.74 us (1%)
  between operations  0.67 us (1%)
    all_to_all x1, blocking collectives, sum_over_chips(): part = lax.all_to_all(part, far, 0, 0, axis_index_groups=turned)  17.2 us
    all_to_all x1, blocking collectives, sum_over_chips(): return lax.all_to_all(part, near, 0, 0)  12 us
    ppermute x2, starting transfers between devices, partners(): return lax.ppermute(value, 'core', [(0, 1), (1, 0)])  10.7 us
    pallas_call x1, Pallas kernels, finish(): pl.pallas_call(functools.partial(finish_kernel, points), in_specs=[smem,...  9.11 us
    all_to_all x1, blocking collectives, sum_over_chips(): part = lax.all_to_all(part, near, 0, 0, axis_index_groups=near_turned)  8.23 us
    pallas_call x1, Pallas kernels, weigh(): pl.pallas_call(weigh_kernel, in_specs=[pl.BlockSpec(memory_space=pltpu.SM...  1.29 us
  transfers between devices with their start and end apart: 2, of which 1 were waited for; matrix products, arithmetic and copies ran while one was open for 0% of the time, Pallas kernels for 2%

profile of v6, /device:TPU:1, one launch (start us, length us, event | category | flops | bytes accessed | tf_op | source)
XLA Modules:
  0.0 60.9 jit_solution(11714498461488046688)
XLA Ops:
  0.6 8.8 %collective-permute-start = (bf16[8192,128]{1,0:T(8,128)(2,1)}, bf16[8192,128]{1,0:T(8,128)(2,1)S(1)}, u32[]{:S(2)}, u32[]{:S(2)}) collective-permute-start(bf16[8192,128]{1,0:T(8,128)(2,1)} %bitcast.3), channel_id=1, source_target_pairs={{0,64},{64,0},{1,65},{65,1},{2,66},{66,2},{3,67},{67,3},{4,68},{68... | collective-permute-start | bytes 6291464 | tf_op jit(solution)/shard_map/ppermute | solution.py:233
  9.4 1.9 %collective-permute-start.1 = (f32[1,128]{1,0:T(1,128)}, f32[1,128]{1,0:T(1,128)S(1)}, u32[]{:S(2)}, u32[]{:S(2)}) collective-permute-start(f32[1,128]{1,0:T(1,128)} %weights_hbm.3), channel_id=1, source_target_pairs={{0,64},{64,0},{1,65},{65,1},{2,66},{66,2},{3,67},{67,3},{4,68},{68... | collective-permute-start | bytes 1544 | tf_op jit(solution)/shard_map/ppermute | solution.py:233
  11.4 1.3 %shard_map.41.own_ref = bf16[4096,128]{1,0:T(8,128)(2,1)S(1)} custom-call(s32[1]{0:T(128)} %bitcast.core_ref, f32[1,128]{1,0:T(1,128)} %weights_hbm.3, bf16[8192,128]{1,0:T(8,128)(2,1)} %bitcast.4), custom_call_target="tpu_custom_call" | custom-call | tf_op jit(solution)/shard_map/pallas_call | solution.py:165
  12.7 0.7 %collective-permute-done.1.other_weights_ref = f32[1,128]{1,0:T(1,128)S(1)} collective-permute-done((f32[1,128]{1,0:T(1,128)}, f32[1,128]{1,0:T(1,128)S(1)}, u32[]{:S(2)}, u32[]{:S(2)}) %collective-permute-start.1) | collective-permute-done | bytes 544 | tf_op jit(solution)/shard_map/ppermute | solution.py:233
  13.4 0.0 collective-permute-done.others_ref
  13.4 0.8 %shard_map.42 = f32[16,9,2,128]{3,2,1,0:T(2,128)S(1)} custom-call(s32[1]{0:T(128)} %bitcast.core_ref, bf16[4096,128]{1,0:T(8,128)(2,1)S(1)} %shard_map.41.own_ref, bf16[8192,128]{1,0:T(8,128)(2,1)S(1)} %collective-permute-done.others_ref, f32[1,128]{1,0:T(1,128)S(1)} %collective-permute-done.1.other_weights_ref), custom_call_target="tpu_custom_call" | custom-call | tf_op jit(solution)/shard_map/pallas_call | solution.py:206
  14.2 8.2 %all_to_all.15 = f32[16,9,2,128]{3,2,1,0:T(2,128)S(1)} all-to-all(f32[16,9,2,128]{3,2,1,0:T(2,128)S(1)} %shard_map.42), channel_id=1, replica_groups={{66,67,68,69,70,71,0,1,2,3,4,5,6,7,64,65},{74,75,76,77,78,79,8,9,10,11,..., dimensions={0} | all-to-all | bytes 294912 | tf_op jit(solution)/shard_map/all_to_all | solution.py:220
  22.4 0.1 reduce_sum.18
  22.5 17.2 %all_to_all.16 = f32[8,9,2,128]{3,2,1,0:T(2,128)S(1)} all-to-all(f32[8,9,2,128]{3,2,1,0:T(2,128)S(1)} %broadcast_in_dim.9), channel_id=1, replica_groups={{32,40,48,56,0,8,16,24},{33,41,49,57,1,9,17,25},{34,42,50,58,2,10,18,26..., dimensions={0} | all-to-all | bytes 147456 | tf_op jit(solution)/shard_map/all_to_all | solution.py:222
  39.8 12.0 %all_to_all.17.gram_ref = f32[16,9,2,128]{3,2,1,0:T(2,128)S(1)} all-to-all(f32[16,9,2,128]{3,2,1,0:T(2,128)S(1)} %broadcast_in_dim.10), channel_id=1, replica_groups=mesh['y'=4,'core'=2,'z_hi'=8,'z_lo'=2,'x'=4] {'core','z_lo','x'}, dimensions={0} | all-to-all | bytes 294912 | tf_op jit(solution)/shard_map/all_to_all | solution.py:224
  51.8 9.1 %shard_map.43 = (bf16[8192,128]{1,0:T(8,128)(2,1)}, f32[1,128]{1,0:T(1,128)}) custom-call(s32[1]{0:T(128)} %bitcast.core_ref, f32[16,9,2,128]{3,2,1,0:T(2,128)S(1)} %all_to_all.17.gram_ref, f32[1,128]{1,0:T(1,128)S(1)} %collective-permute-done.1.other_weights_ref, f32[1,128]{1,0:T(1,128)} %weights_hbm.3, bf16[8192,128]{1,0:T(8,128)(2,1)} %bitcast.5, ...), custom_call_target="tpu_custom_call" | custom-call | tf_op jit(solution)/shard_map/pallas_call | solution.py:126
  (3 shorter events, 0.1 us)
Async XLA Ops:
  0.6 12.8 %collective-permute-start = (bf16[8192,128]{1,0:T(8,128)(2,1)}, bf16[8192,128]{1,0:T(8,128)(2,1)S(1)}, u32[]{:S(2)}, u32[]{:S(2)}) collective-permute-start(bf16[8192,128]{1,0:T(8,128)(2,1)} %bitcast.3), channel_id=1, source_target_pairs={{0,64},{64,0},{1,65},{65,1},{2,66},{66,2},{3,67},{67,3},{4,68},{68... | collective-permute-start | bytes 6291464 | tf_op jit(solution)/shard_map/ppermute | solution.py:233
  9.4 4.0 %collective-permute-start.1 = (f32[1,128]{1,0:T(1,128)}, f32[1,128]{1,0:T(1,128)S(1)}, u32[]{:S(2)}, u32[]{:S(2)}) collective-permute-start(f32[1,128]{1,0:T(1,128)} %weights_hbm.3), channel_id=1, source_target_pairs={{0,64},{64,0},{1,65},{65,1},{2,66},{66,2},{3,67},{67,3},{4,68},{68... | collective-permute-start | bytes 1544 | tf_op jit(solution)/shard_map/ppermute | solution.py:233

commit v7 on v6

--- a/solution.py
+++ b/solution.py
@@ -12,6 +12,8 @@
 NS_STEPS = 6
 CHUNK = 1024
 FIRST = 10
+FAR_FIRST = 5
+GATHER_FIRST = 14
 ROWS = (((0,), (0,)), ((), ()))
 PLAIN = (((1,), (0,)), ((), ()))
 COLUMNS = (((1,), (1,)), ((), ()))
@@ -87,7 +89,7 @@
     for k in range(slices):
         for p in range(pairs - 1):
             first = k * each + 2 * p if 2 * p < each else w + k * each + 2 * p - each
-            gram_rows_ref[first : first + 2] = gram_ref[k, p]
+            gram_rows_ref[first : first + 2] = gram_ref[(k - GATHER_FIRST) % slices, p]
     shared, ab = gram_rows_ref[:w], gram_rows_ref[w:]
     turned = shared.T
     row = lax.broadcasted_iota(jnp.int32, (w, w), 0)
@@ -215,13 +217,15 @@
 def sum_over_chips(part):
     near, far = ("core", "z_lo", "x"), "z_hi"
     n, m = part.shape[0], lax.axis_size(far)
-    turned = [[(i + m // 2) % m for i in range(m)]]
-    near_turned = [[(i + FIRST) % n for i in range(n)]]
-    part = lax.all_to_all(part, near, 0, 0, axis_index_groups=near_turned)
+
+    def turned(size, first):
+        return [[(i + first) % size for i in range(size)]]
+
+    part = lax.all_to_all(part, near, 0, 0, axis_index_groups=turned(n, FIRST))
     part = jnp.broadcast_to(jnp.sum(part, axis=0)[None], (m, *part.shape[1:]))
-    part = lax.all_to_all(part, far, 0, 0, axis_index_groups=turned)
+    part = lax.all_to_all(part, far, 0, 0, axis_index_groups=turned(m, FAR_FIRST))
     part = jnp.broadcast_to(jnp.sum(part, axis=0)[None], (n, *part.shape[1:]))
-    return lax.all_to_all(part, near, 0, 0)
+    return lax.all_to_all(part, near, 0, 0, axis_index_groups=turned(n, GATHER_FIRST))
 
 
 def local(bases, sing_values):

time: 61.2 us -> 58.5 us (0.956)
  blocking collectives: 37.4 us -> 34.8 us
    all_to_all x3, blocking collectives: 37.4 us -> 34.8 us  [the longest x1 16 us: sum_over_chips(): lax.all_to_all(part, far, 0, 0, axis_index_groups=turned(m, FAR_FIRST))]
where the time goes in v7:
time: 58.5 us; the launch traced here: 58.3 us
  blocking collectives  34.8 us (59%)
  Pallas kernels  11.2 us (19%)
  starting transfers between devices  10.7 us (18%)
  waiting for transfers between devices  0.74 us (1%)
  between operations  0.67 us (1%)
    all_to_all x1, blocking collectives, sum_over_chips(): lax.all_to_all(part, far, 0, 0, axis_index_groups=turned(m, FAR_FIRST))  16 us
    ppermute x2, starting transfers between devices, partners(): return lax.ppermute(value, 'core', [(0, 1), (1, 0)])  10.7 us
    all_to_all x1, blocking collectives, sum_over_chips(): lax.all_to_all(part, near, 0, 0, axis_index_groups=turned(n, GATHER_FIRST))  10.5 us
    pallas_call x1, Pallas kernels, finish(): pl.pallas_call(functools.partial(finish_kernel, points), in_specs=[smem,...  9.12 us
    all_to_all x1, blocking collectives, sum_over_chips(): part = lax.all_to_all(part, near, 0, 0, axis_index_groups=turned(n, FIRST))  8.23 us
    pallas_call x1, Pallas kernels, weigh(): pl.pallas_call(weigh_kernel, in_specs=[pl.BlockSpec(memory_space=pltpu.SM...  1.29 us
  transfers between devices with their start and end apart: 2, of which 1 were waited for; matrix products, arithmetic and copies ran while one was open for 0% of the time, Pallas kernels for 2%

profile of v7, /device:TPU:1, one launch (start us, length us, event | category | flops | bytes accessed | tf_op | source)
XLA Modules:
  0.0 58.3 jit_solution(8541367992187839199)
XLA Ops:
  0.6 8.8 %collective-permute-start = (bf16[8192,128]{1,0:T(8,128)(2,1)}, bf16[8192,128]{1,0:T(8,128)(2,1)S(1)}, u32[]{:S(2)}, u32[]{:S(2)}) collective-permute-start(bf16[8192,128]{1,0:T(8,128)(2,1)} %bitcast.3), channel_id=1, source_target_pairs={{0,64},{64,0},{1,65},{65,1},{2,66},{66,2},{3,67},{67,3},{4,68},{68... | collective-permute-start | bytes 6291464 | tf_op jit(solution)/shard_map/ppermute | solution.py:237
  9.4 1.9 %collective-permute-start.1 = (f32[1,128]{1,0:T(1,128)}, f32[1,128]{1,0:T(1,128)S(1)}, u32[]{:S(2)}, u32[]{:S(2)}) collective-permute-start(f32[1,128]{1,0:T(1,128)} %weights_hbm.3), channel_id=1, source_target_pairs={{0,64},{64,0},{1,65},{65,1},{2,66},{66,2},{3,67},{67,3},{4,68},{68... | collective-permute-start | bytes 1544 | tf_op jit(solution)/shard_map/ppermute | solution.py:237
  11.4 1.3 %shard_map.41.own_ref = bf16[4096,128]{1,0:T(8,128)(2,1)S(1)} custom-call(s32[1]{0:T(128)} %bitcast.core_ref, f32[1,128]{1,0:T(1,128)} %weights_hbm.3, bf16[8192,128]{1,0:T(8,128)(2,1)} %bitcast.4), custom_call_target="tpu_custom_call" | custom-call | tf_op jit(solution)/shard_map/pallas_call | solution.py:167
  12.7 0.7 %collective-permute-done.1.other_weights_ref = f32[1,128]{1,0:T(1,128)S(1)} collective-permute-done((f32[1,128]{1,0:T(1,128)}, f32[1,128]{1,0:T(1,128)S(1)}, u32[]{:S(2)}, u32[]{:S(2)}) %collective-permute-start.1) | collective-permute-done | bytes 544 | tf_op jit(solution)/shard_map/ppermute | solution.py:237
  13.4 0.0 collective-permute-done.others_ref
  13.4 0.8 %shard_map.42 = f32[16,9,2,128]{3,2,1,0:T(2,128)S(1)} custom-call(s32[1]{0:T(128)} %bitcast.core_ref, bf16[4096,128]{1,0:T(8,128)(2,1)S(1)} %shard_map.41.own_ref, bf16[8192,128]{1,0:T(8,128)(2,1)S(1)} %collective-permute-done.others_ref, f32[1,128]{1,0:T(1,128)S(1)} %collective-permute-done.1.other_weights_ref), custom_call_target="tpu_custom_call" | custom-call | tf_op jit(solution)/shard_map/pallas_call | solution.py:208
  14.2 8.2 %all_to_all.15 = f32[16,9,2,128]{3,2,1,0:T(2,128)S(1)} all-to-all(f32[16,9,2,128]{3,2,1,0:T(2,128)S(1)} %shard_map.42), channel_id=1, replica_groups={{66,67,68,69,70,71,0,1,2,3,4,5,6,7,64,65},{74,75,76,77,78,79,8,9,10,11,..., dimensions={0} | all-to-all | bytes 294912 | tf_op jit(solution)/shard_map/all_to_all | solution.py:224
  22.4 0.1 reduce_sum.18
  22.5 16.0 %all_to_all.16 = f32[8,9,2,128]{3,2,1,0:T(2,128)S(1)} all-to-all(f32[8,9,2,128]{3,2,1,0:T(2,128)S(1)} %broadcast_in_dim.9), channel_id=1, replica_groups={{40,48,56,0,8,16,24,32},{41,49,57,1,9,17,25,33},{42,50,58,2,10,18,26,34..., dimensions={0} | all-to-all | bytes 147456 | tf_op jit(solution)/shard_map/all_to_all | solution.py:226
  38.6 10.5 %all_to_all.17.gram_ref = f32[16,9,2,128]{3,2,1,0:T(2,128)S(1)} all-to-all(f32[16,9,2,128]{3,2,1,0:T(2,128)S(1)} %broadcast_in_dim.10), channel_id=1, replica_groups={{70,71,0,1,2,3,4,5,6,7,64,65,66,67,68,69},{78,79,8,9,10,11,12,13,14,15,..., dimensions={0} | all-to-all | bytes 294912 | tf_op jit(solution)/shard_map/all_to_all | solution.py:228
  49.1 9.1 %shard_map.43 = (bf16[8192,128]{1,0:T(8,128)(2,1)}, f32[1,128]{1,0:T(1,128)}) custom-call(s32[1]{0:T(128)} %bitcast.core_ref, f32[16,9,2,128]{3,2,1,0:T(2,128)S(1)} %all_to_all.17.gram_ref, f32[1,128]{1,0:T(1,128)S(1)} %collective-permute-done.1.other_weights_ref, f32[1,128]{1,0:T(1,128)} %weights_hbm.3, bf16[8192,128]{1,0:T(8,128)(2,1)} %bitcast.5, ...), custom_call_target="tpu_custom_call" | custom-call | tf_op jit(solution)/shard_map/pallas_call | solution.py:128
  (3 shorter events, 0.1 us)
Async XLA Ops:
  0.6 12.8 %collective-permute-start = (bf16[8192,128]{1,0:T(8,128)(2,1)}, bf16[8192,128]{1,0:T(8,128)(2,1)S(1)}, u32[]{:S(2)}, u32[]{:S(2)}) collective-permute-start(bf16[8192,128]{1,0:T(8,128)(2,1)} %bitcast.3), channel_id=1, source_target_pairs={{0,64},{64,0},{1,65},{65,1},{2,66},{66,2},{3,67},{67,3},{4,68},{68... | collective-permute-start | bytes 6291464 | tf_op jit(solution)/shard_map/ppermute | solution.py:237
  9.4 4.0 %collective-permute-start.1 = (f32[1,128]{1,0:T(1,128)}, f32[1,128]{1,0:T(1,128)S(1)}, u32[]{:S(2)}, u32[]{:S(2)}) collective-permute-start(f32[1,128]{1,0:T(1,128)} %weights_hbm.3), channel_id=1, source_target_pairs={{0,64},{64,0},{1,65},{65,1},{2,66},{66,2},{3,67},{67,3},{4,68},{68... | collective-permute-start | bytes 1544 | tf_op jit(solution)/shard_map/ppermute | solution.py:237

commit v8 on v7

--- a/solution.py
+++ b/solution.py
@@ -84,18 +84,18 @@
     ]
     for load in loads:
         load.start()
-    slices, pairs = gram_ref.shape[:2]
+    slices, lines = gram_ref.shape[:2]
     each = w // slices
     for k in range(slices):
-        for p in range(pairs - 1):
-            first = k * each + 2 * p if 2 * p < each else w + k * each + 2 * p - each
-            gram_rows_ref[first : first + 2] = gram_ref[(k - GATHER_FIRST) % slices, p]
+        for p in range(lines - 1):
+            first = k * each + p if p < each else w + k * each + p - each
+            gram_rows_ref[first : first + 1] = gram_ref[(k - GATHER_FIRST) % slices, p]
     shared, ab = gram_rows_ref[:w], gram_rows_ref[w:]
     turned = shared.T
     row = lax.broadcasted_iota(jnp.int32, (w, w), 0)
     column = lax.broadcasted_iota(jnp.int32, (w, w), 1)
     aa = jnp.where(row <= column, shared, turned)
-    bb = jnp.where(row > column, shared, jnp.where(row < column, turned, gram_ref[0, pairs - 1, :1]))
+    bb = jnp.where(row > column, shared, jnp.where(row < column, turned, gram_ref[0, lines - 1]))
     gram = jnp.concatenate(
         [jnp.concatenate([aa, ab], axis=1), jnp.concatenate([ab.T, bb], axis=1)], axis=0
     )
@@ -192,14 +192,14 @@
     column = lax.broadcasted_iota(jnp.int32, (w, w), 1)
     shared = jnp.where(row <= column, aa, bb)
     diag = jnp.sum(jnp.where(row == column, bb, 0.0), axis=0, keepdims=True)
-    slices, pairs = out_ref.shape[:2]
+    slices, lines = out_ref.shape[:2]
     each = w // slices
     for k in range(slices):
-        for p in range(each // 2):
-            first = k * each + 2 * p
-            out_ref[(k - FIRST) % slices, p] = shared[first : first + 2]
-            out_ref[(k - FIRST) % slices, each // 2 + p] = across[first : first + 2]
-        out_ref[k, pairs - 1] = jnp.broadcast_to(diag, (2, w))
+        for p in range(each):
+            first = k * each + p
+            out_ref[(k - FIRST) % slices, p] = shared[first : first + 1]
+            out_ref[(k - FIRST) % slices, each + p] = across[first : first + 1]
+        out_ref[k, lines - 1] = diag
 
 
 def half_gram(core, own, others, other_values, slices):
@@ -209,7 +209,7 @@
         gram_kernel,
         in_specs=[pl.BlockSpec(memory_space=pltpu.SMEM)] + [vmem] * 3,
         out_specs=vmem,
-        out_shape=jax.ShapeDtypeStruct((slices, w // slices + 1, 2, w), f32),
+        out_shape=jax.ShapeDtypeStruct((slices, 2 * (w // slices) + 1, 1, w), f32),
         compiler_params=pltpu.CompilerParams(vmem_limit_bytes=12 << 20),
     )(core, own, others, other_values)
 

time: 58.5 us -> 58.3 us (level)
    all_to_all x1, blocking collectives: 10.5 us -> 9.59 us  [sum_over_chips(): lax.all_to_all(part, near, 0, 0, axis_index_groups=turned(n, GATHER_FIRST))]
    all_to_all x1, blocking collectives: 16 us -> 16.7 us  [sum_over_chips(): lax.all_to_all(part, far, 0, 0, axis_index_groups=turned(m, FAR_FIRST))]
where the time goes in v8:
time: 58.3 us; the launch traced here: 58 us
  blocking collectives  34.5 us (59%)
  Pallas kernels  11.2 us (19%)
  starting transfers between devices  10.7 us (18%)
  waiting for transfers between devices  0.74 us (1%)
  between operations  0.69 us (1%)
    all_to_all x1, blocking collectives, sum_over_chips(): lax.all_to_all(part, far, 0, 0, axis_index_groups=turned(m, FAR_FIRST))  16.7 us
    ppermute x2, starting transfers between devices, partners(): return lax.ppermute(value, 'core', [(0, 1), (1, 0)])  10.7 us
    all_to_all x1, blocking collectives, sum_over_chips(): lax.all_to_all(part, near, 0, 0, axis_index_groups=turned(n, GATHER_FIRST))  9.59 us
    pallas_call x1, Pallas kernels, finish(): pl.pallas_call(functools.partial(finish_kernel, points), in_specs=[smem,...  9.12 us
    all_to_all x1, blocking collectives, sum_over_chips(): part = lax.all_to_all(part, near, 0, 0, axis_index_groups=turned(n, FIRST))  8.14 us
    pallas_call x1, Pallas kernels, weigh(): pl.pallas_call(weigh_kernel, in_specs=[pl.BlockSpec(memory_space=pltpu.SM...  1.29 us
  transfers between devices with their start and end apart: 2, of which 1 were waited for; matrix products, arithmetic and copies ran while one was open for 0% of the time, Pallas kernels for 2%

profile of v8, /device:TPU:1, one launch (start us, length us, event | category | flops | bytes accessed | tf_op | source)
XLA Modules:
  0.0 58.0 jit_solution(2469828233890257474)
XLA Ops:
  0.6 8.8 %collective-permute-start = (bf16[8192,128]{1,0:T(8,128)(2,1)}, bf16[8192,128]{1,0:T(8,128)(2,1)S(1)}, u32[]{:S(2)}, u32[]{:S(2)}) collective-permute-start(bf16[8192,128]{1,0:T(8,128)(2,1)} %bitcast.3), channel_id=1, source_target_pairs={{0,64},{64,0},{1,65},{65,1},{2,66},{66,2},{3,67},{67,3},{4,68},{68... | collective-permute-start | bytes 6291464 | tf_op jit(solution)/shard_map/ppermute | solution.py:237
  9.4 1.9 %collective-permute-start.1 = (f32[1,128]{1,0:T(1,128)}, f32[1,128]{1,0:T(1,128)S(1)}, u32[]{:S(2)}, u32[]{:S(2)}) collective-permute-start(f32[1,128]{1,0:T(1,128)} %weights_hbm.3), channel_id=1, source_target_pairs={{0,64},{64,0},{1,65},{65,1},{2,66},{66,2},{3,67},{67,3},{4,68},{68... | collective-permute-start | bytes 1544 | tf_op jit(solution)/shard_map/ppermute | solution.py:237
  11.4 1.3 %shard_map.41.own_ref = bf16[4096,128]{1,0:T(8,128)(2,1)S(1)} custom-call(s32[1]{0:T(128)} %bitcast.core_ref, f32[1,128]{1,0:T(1,128)} %weights_hbm.3, bf16[8192,128]{1,0:T(8,128)(2,1)} %bitcast.4), custom_call_target="tpu_custom_call" | custom-call | tf_op jit(solution)/shard_map/pallas_call | solution.py:167
  12.7 0.7 %collective-permute-done.1.other_weights_ref = f32[1,128]{1,0:T(1,128)S(1)} collective-permute-done((f32[1,128]{1,0:T(1,128)}, f32[1,128]{1,0:T(1,128)S(1)}, u32[]{:S(2)}, u32[]{:S(2)}) %collective-permute-start.1) | collective-permute-done | bytes 544 | tf_op jit(solution)/shard_map/ppermute | solution.py:237
  13.4 0.0 collective-permute-done.others_ref
  13.4 0.8 %shard_map.42 = f32[16,17,1,128]{3,2,1,0:T(1,128)S(1)} custom-call(s32[1]{0:T(128)} %bitcast.core_ref, bf16[4096,128]{1,0:T(8,128)(2,1)S(1)} %shard_map.41.own_ref, bf16[8192,128]{1,0:T(8,128)(2,1)S(1)} %collective-permute-done.others_ref, f32[1,128]{1,0:T(1,128)S(1)} %collective-permute-done.1.other_weights_ref), custom_call_target="tpu_custom_call" | custom-call | tf_op jit(solution)/shard_map/pallas_call | solution.py:208
  14.2 8.1 %all_to_all.15 = f32[16,17,1,128]{3,2,1,0:T(1,128)S(1)} all-to-all(f32[16,17,1,128]{3,2,1,0:T(1,128)S(1)} %shard_map.42), channel_id=1, replica_groups={{66,67,68,69,70,71,0,1,2,3,4,5,6,7,64,65},{74,75,76,77,78,79,8,9,10,11,..., dimensions={0} | all-to-all | bytes 278528 | tf_op jit(solution)/shard_map/all_to_all | solution.py:224
  22.3 0.1 reduce_sum.18
  22.5 16.7 %all_to_all.16 = f32[8,17,1,128]{3,2,1,0:T(1,128)S(1)} all-to-all(f32[8,17,1,128]{3,2,1,0:T(1,128)S(1)} %broadcast_in_dim.9), channel_id=1, replica_groups={{40,48,56,0,8,16,24,32},{41,49,57,1,9,17,25,33},{42,50,58,2,10,18,26,34..., dimensions={0} | all-to-all | bytes 139264 | tf_op jit(solution)/shard_map/all_to_all | solution.py:226
  39.2 0.1 reduce_sum.19
  39.3 0.1 broadcast_in_dim.10
  39.3 9.6 %all_to_all.17.gram_ref = f32[16,17,1,128]{3,2,1,0:T(1,128)S(1)} all-to-all(f32[16,17,1,128]{3,2,1,0:T(1,128)S(1)} %broadcast_in_dim.10), channel_id=1, replica_groups={{70,71,0,1,2,3,4,5,6,7,64,65,66,67,68,69},{78,79,8,9,10,11,12,13,14,15,..., dimensions={0} | all-to-all | bytes 278528 | tf_op jit(solution)/shard_map/all_to_all | solution.py:228
  48.9 9.1 %shard_map.43 = (bf16[8192,128]{1,0:T(8,128)(2,1)}, f32[1,128]{1,0:T(1,128)}) custom-call(s32[1]{0:T(128)} %bitcast.core_ref, f32[16,17,1,128]{3,2,1,0:T(1,128)S(1)} %all_to_all.17.gram_ref, f32[1,128]{1,0:T(1,128)S(1)} %collective-permute-done.1.other_weights_ref, f32[1,128]{1,0:T(1,128)} %weights_hbm.3, bf16[8192,128]{1,0:T(8,128)(2,1)} %bitcast.5, ...), custom_call_target="tpu_custom_call" | custom-call | tf_op jit(solution)/shard_map/pallas_call | solution.py:128
  (1 shorter events, 0.0 us)
Async XLA Ops:
  0.6 12.8 %collective-permute-start = (bf16[8192,128]{1,0:T(8,128)(2,1)}, bf16[8192,128]{1,0:T(8,128)(2,1)S(1)}, u32[]{:S(2)}, u32[]{:S(2)}) collective-permute-start(bf16[8192,128]{1,0:T(8,128)(2,1)} %bitcast.3), channel_id=1, source_target_pairs={{0,64},{64,0},{1,65},{65,1},{2,66},{66,2},{3,67},{67,3},{4,68},{68... | collective-permute-start | bytes 6291464 | tf_op jit(solution)/shard_map/ppermute | solution.py:237
  9.4 4.0 %collective-permute-start.1 = (f32[1,128]{1,0:T(1,128)}, f32[1,128]{1,0:T(1,128)S(1)}, u32[]{:S(2)}, u32[]{:S(2)}) collective-permute-start(f32[1,128]{1,0:T(1,128)} %weights_hbm.3), channel_id=1, source_target_pairs={{0,64},{64,0},{1,65},{65,1},{2,66},{66,2},{3,67},{67,3},{4,68},{68... | collective-permute-start | bytes 1544 | tf_op jit(solution)/shard_map/ppermute | solution.py:237

commit v9 on v8

--- a/solution.py
+++ b/solution.py
@@ -10,7 +10,7 @@
 
 ITERS = 3
 NS_STEPS = 6
-CHUNK = 1024
+CHUNK = 512
 FIRST = 10
 FAR_FIRST = 5
 GATHER_FIRST = 14
@@ -46,11 +46,12 @@
         m = wide_dot(yt, yt, COLUMNS) * scale
         yt = yt * jnp.sqrt(scale)
         last = outer == ITERS - 1
-        ahead = yt.T if last else wide_dot(yt, gram)
         square = wide_dot(m, m)
         q = 1.5 * diag.astype(f32) - 0.5 * m
         for inner in range(1, NS_STEPS):
             m = 2.25 * m - 1.5 * square + 0.25 * wide_dot(square, m)
+            if inner == NS_STEPS // 2:
+                ahead = yt.T if last else wide_dot(yt, gram)
             if inner < NS_STEPS - 1:
                 both = wide_dot(jnp.concatenate([m, q], axis=0), m)
                 square = both[:w]

time: 58.3 us -> 58.3 us (level)
  no operation moved by 1% of the time
where the time goes in v9:
time: 58.3 us; the launch traced here: 58 us
  blocking collectives  34.5 us (59%)
  Pallas kernels  11.2 us (19%)
  starting transfers between devices  10.7 us (18%)
  between operations  0.69 us (1%)
  waiting for transfers between devices  0.63 us (1%)
    all_to_all x1, blocking collectives, sum_over_chips(): lax.all_to_all(part, far, 0, 0, axis_index_groups=turned(m, FAR_FIRST))  16.7 us
    ppermute x2, starting transfers between devices, partners(): return lax.ppermute(value, 'core', [(0, 1), (1, 0)])  10.7 us
    all_to_all x1, blocking collectives, sum_over_chips(): lax.all_to_all(part, near, 0, 0, axis_index_groups=turned(n, GATHER_FIRST))  9.59 us
    pallas_call x1, Pallas kernels, finish(): pl.pallas_call(functools.partial(finish_kernel, points), in_specs=[smem,...  9.06 us
    all_to_all x1, blocking collectives, sum_over_chips(): part = lax.all_to_all(part, near, 0, 0, axis_index_groups=turned(n, FIRST))  8.14 us
    pallas_call x1, Pallas kernels, weigh(): pl.pallas_call(weigh_kernel, in_specs=[pl.BlockSpec(memory_space=pltpu.SM...  1.4 us
  transfers between devices with their start and end apart: 2, of which 1 were waited for; matrix products, arithmetic and copies ran while one was open for 0% of the time, Pallas kernels for 2%

profile of v9, /device:TPU:1, one launch (start us, length us, event | category | flops | bytes accessed | tf_op | source)
XLA Modules:
  0.0 58.0 jit_solution(173164741138027462)
XLA Ops:
  0.6 8.8 %collective-permute-start = (bf16[8192,128]{1,0:T(8,128)(2,1)}, bf16[8192,128]{1,0:T(8,128)(2,1)S(1)}, u32[]{:S(2)}, u32[]{:S(2)}) collective-permute-start(bf16[8192,128]{1,0:T(8,128)(2,1)} %bitcast.3), channel_id=1, source_target_pairs={{0,64},{64,0},{1,65},{65,1},{2,66},{66,2},{3,67},{67,3},{4,68},{68... | collective-permute-start | bytes 6291464 | tf_op jit(solution)/shard_map/ppermute | solution.py:238
  9.4 1.9 %collective-permute-start.1 = (f32[1,128]{1,0:T(1,128)}, f32[1,128]{1,0:T(1,128)S(1)}, u32[]{:S(2)}, u32[]{:S(2)}) collective-permute-start(f32[1,128]{1,0:T(1,128)} %weights_hbm.3), channel_id=1, source_target_pairs={{0,64},{64,0},{1,65},{65,1},{2,66},{66,2},{3,67},{67,3},{4,68},{68... | collective-permute-start | bytes 1544 | tf_op jit(solution)/shard_map/ppermute | solution.py:238
  11.4 1.4 %shard_map.41.own_ref = bf16[4096,128]{1,0:T(8,128)(2,1)S(1)} custom-call(s32[1]{0:T(128)} %bitcast.core_ref, f32[1,128]{1,0:T(1,128)} %weights_hbm.3, bf16[8192,128]{1,0:T(8,128)(2,1)} %bitcast.4), custom_call_target="tpu_custom_call" | custom-call | tf_op jit(solution)/shard_map/pallas_call | solution.py:168
  12.8 0.6 %collective-permute-done.1.other_weights_ref = f32[1,128]{1,0:T(1,128)S(1)} collective-permute-done((f32[1,128]{1,0:T(1,128)}, f32[1,128]{1,0:T(1,128)S(1)}, u32[]{:S(2)}, u32[]{:S(2)}) %collective-permute-start.1) | collective-permute-done | bytes 544 | tf_op jit(solution)/shard_map/ppermute | solution.py:238
  13.4 0.0 collective-permute-done.others_ref
  13.4 0.8 %shard_map.42 = f32[16,17,1,128]{3,2,1,0:T(1,128)S(1)} custom-call(s32[1]{0:T(128)} %bitcast.core_ref, bf16[4096,128]{1,0:T(8,128)(2,1)S(1)} %shard_map.41.own_ref, bf16[8192,128]{1,0:T(8,128)(2,1)S(1)} %collective-permute-done.others_ref, f32[1,128]{1,0:T(1,128)S(1)} %collective-permute-done.1.other_weights_ref), custom_call_target="tpu_custom_call" | custom-call | tf_op jit(solution)/shard_map/pallas_call | solution.py:209
  14.2 8.1 %all_to_all.15 = f32[16,17,1,128]{3,2,1,0:T(1,128)S(1)} all-to-all(f32[16,17,1,128]{3,2,1,0:T(1,128)S(1)} %shard_map.42), channel_id=1, replica_groups={{66,67,68,69,70,71,0,1,2,3,4,5,6,7,64,65},{74,75,76,77,78,79,8,9,10,11,..., dimensions={0} | all-to-all | bytes 278528 | tf_op jit(solution)/shard_map/all_to_all | solution.py:225
  22.3 0.1 reduce_sum.18
  22.5 16.7 %all_to_all.16 = f32[8,17,1,128]{3,2,1,0:T(1,128)S(1)} all-to-all(f32[8,17,1,128]{3,2,1,0:T(1,128)S(1)} %broadcast_in_dim.9), channel_id=1, replica_groups={{40,48,56,0,8,16,24,32},{41,49,57,1,9,17,25,33},{42,50,58,2,10,18,26,34..., dimensions={0} | all-to-all | bytes 139264 | tf_op jit(solution)/shard_map/all_to_all | solution.py:227
  39.2 0.1 reduce_sum.19
  39.3 0.1 broadcast_in_dim.10
  39.3 9.6 %all_to_all.17.gram_ref = f32[16,17,1,128]{3,2,1,0:T(1,128)S(1)} all-to-all(f32[16,17,1,128]{3,2,1,0:T(1,128)S(1)} %broadcast_in_dim.10), channel_id=1, replica_groups={{70,71,0,1,2,3,4,5,6,7,64,65,66,67,68,69},{78,79,8,9,10,11,12,13,14,15,..., dimensions={0} | all-to-all | bytes 278528 | tf_op jit(solution)/shard_map/all_to_all | solution.py:229
  48.9 9.1 %shard_map.43 = (bf16[8192,128]{1,0:T(8,128)(2,1)}, f32[1,128]{1,0:T(1,128)}) custom-call(s32[1]{0:T(128)} %bitcast.core_ref, f32[16,17,1,128]{3,2,1,0:T(1,128)S(1)} %all_to_all.17.gram_ref, f32[1,128]{1,0:T(1,128)S(1)} %collective-permute-done.1.other_weights_ref, f32[1,128]{1,0:T(1,128)} %weights_hbm.3, bf16[8192,128]{1,0:T(8,128)(2,1)} %bitcast.5, ...), custom_call_target="tpu_custom_call" | custom-call | tf_op jit(solution)/shard_map/pallas_call | solution.py:129
  (1 shorter events, 0.0 us)
Async XLA Ops:
  0.6 12.8 %collective-permute-start = (bf16[8192,128]{1,0:T(8,128)(2,1)}, bf16[8192,128]{1,0:T(8,128)(2,1)S(1)}, u32[]{:S(2)}, u32[]{:S(2)}) collective-permute-start(bf16[8192,128]{1,0:T(8,128)(2,1)} %bitcast.3), channel_id=1, source_target_pairs={{0,64},{64,0},{1,65},{65,1},{2,66},{66,2},{3,67},{67,3},{4,68},{68... | collective-permute-start | bytes 6291464 | tf_op jit(solution)/shard_map/ppermute | solution.py:238
  9.4 4.0 %collective-permute-start.1 = (f32[1,128]{1,0:T(1,128)}, f32[1,128]{1,0:T(1,128)S(1)}, u32[]{:S(2)}, u32[]{:S(2)}) collective-permute-start(f32[1,128]{1,0:T(1,128)} %weights_hbm.3), channel_id=1, source_target_pairs={{0,64},{64,0},{1,65},{65,1},{2,66},{66,2},{3,67},{67,3},{4,68},{68... | collective-permute-start | bytes 1544 | tf_op jit(solution)/shard_map/ppermute | solution.py:238
